TPU v7x, 32 devices: a whole 2x2x4 slice. The times are simulated.
32 devices in a mesh: expert: 4 (over y, x), fsdp: 8 (over z, core).
Axes of the slice: x: 2, y: 2, z: 4, core: 2. Of those that a mesh axis runs over, the one named last changes fastest.
Arguments:
- branch_wo: bfloat16 [4, 4096, 4096], P('expert', 'fsdp'), may hold values from -3 to 3
- context: bfloat16 [1024, 4096], P('fsdp', 'expert'), may hold values from -6 to 6
- residual: bfloat16 [1024, 4096], P('fsdp', 'expert'), may hold values from -160 to 160
- norm_gain: bfloat16 [4096], P('expert'), may hold values from 0.25 to 1.75
- router_w: bfloat16 [4096, 4], P('expert'), may hold values from -0.1875 to 0.1875
- gate_w: bfloat16 [4, 4096, 8192], P('expert', None, 'fsdp'), may hold values from -0.09375 to 0.09375
- up_w: bfloat16 [4, 4096, 8192], P('expert', None, 'fsdp'), may hold values from -0.09375 to 0.09375
- expert_ids: int32 [1024, 2], P('fsdp'), may hold values from 0 to 3, as said below
- slot_ids: int32 [1024, 2], P('fsdp'), may hold values from 0 to 95, as said below
- cot_hidden: bfloat16 [4, 768, 8192], P('expert', None, 'fsdp'), may hold values from -1.1953125 to 1.1953125
Outputs:
- merged_wo: bfloat16 [4096, 4096], P('fsdp', 'expert')
- hidden: bfloat16 [4, 768, 8192], P('expert', None, 'fsdp')
- grad_gate: bfloat16 [4, 4096, 8192], P('expert', None, 'fsdp')
- grad_up: bfloat16 [4, 4096, 8192], P('expert', None, 'fsdp')
Inputs may be any that keep to these rules, and one draw needn't show every extreme that they name: expert_ids[t, 0] and expert_ids[t, 1] differ. Within each aligned block of 128 tokens (the tokens of one index of fsdp) no expert is named more than 96 times, and some expert is named exactly 96 times in every block. Within each aligned block of 128 tokens the pairs (expert_ids[t, k], slot_ids[t, k]) are all different, and an expert named c times in the block uses exactly the slots 0 to c - 1.
All inputs are finite; a program needn't handle non-finite values.
Results may differ from a plain program's by a relative error of at most 0.015.
Values may be sent and summed in bfloat16 or wider, within the bound.
No kernel may reach another device: no remote copies, remote signals or barrier semaphores. Data moves between devices by JAX's collectives and lax.ppermute only.
A program may use at most 128 MiB of HBM per device.

v0:
```python
import functools

import jax
import jax.numpy as jnp
from jax import lax
from jax.experimental import pallas as pl
from jax.experimental.pallas import tpu as pltpu
from jax.sharding import PartitionSpec as P

CHUNKS = 2
MEBI = 1024 * 1024


def exchange(value, axis, offset):
    size = lax.axis_size(axis)
    return lax.ppermute(value, axis, [(i, i ^ offset) for i in range(size)])


def pick(value, index, axis):
    return lax.dynamic_index_in_dim(value, index, axis, keepdims=False)


def after(value, *others):
    return lax.optimization_barrier((value, others))[0]


def bits_of(size):
    return size.bit_length() - 1


def whole(shape):
    return pl.BlockSpec(shape, lambda *_: (0,) * len(shape))


def smem():
    return pl.BlockSpec(memory_space=pltpu.SMEM)


def params(mebi=16):
    return pltpu.CompilerParams(vmem_limit_bytes=mebi * MEBI)


def signs_kernel(experts, position_ref, ids_ref, out_ref):
    blocks, capacity, lanes = out_ref.shape
    tokens = ids_ref.shape[2]
    expert = position_ref[0]
    slots = lax.broadcasted_iota(jnp.int32, (capacity, tokens), 0)
    rows = lax.broadcasted_iota(jnp.int32, (lanes, tokens), 0)
    last = lax.broadcasted_iota(jnp.int32, (capacity, lanes), 1) == lanes - 1
    for b in range(blocks):
        ids = ids_ref[b]
        e0, e1, s0, s1 = ids[0:1], ids[1:2], ids[2:3], ids[3:4]
        hit0 = jnp.where((e0 == expert) & (s0 == slots), 1.0, 0.0)
        hit1 = jnp.where((e1 == expert) & (s1 == slots), 1.0, 0.0)
        table = jnp.where(e0 == rows - 1, 1.0, 0.0) - jnp.where(e1 == rows - 1, 1.0, 0.0)
        signs = lax.dot_general(
            (hit0 - hit1).astype(jnp.bfloat16),
            table.astype(jnp.bfloat16),
            (((1,), (1,)), ((), ())),
            preferred_element_type=jnp.float32,
        )
        filled = jnp.sum(hit0 + hit1, axis=1, keepdims=True)
        out_ref[b] = jnp.where(last, filled, signs)


def pack_kernel(c, flip, position_ref, branch_ref, low_out, high_out, sems):
    others, half, part = low_out.shape
    expert = position_ref[0]
    copies = []
    for j in range(others):
        low = 2 * j + (expert % 2 ^ flip)
        high = j + others * (expert // others ^ flip)
        for h, (place, out) in enumerate(((low, low_out), (high, high_out))):
            columns = pl.ds(pl.multiple_of((place * CHUNKS + c) * part, 128), part)
            source = branch_ref.at[pl.ds(h * half, half), columns]
            copies.append(pltpu.make_async_copy(source, out.at[j], sems.at[2 * j + h]))
    for copy in copies:
        copy.start()
    for copy in copies:
        copy.wait()


def pack(position, branch, c, flip, experts):
    others = experts // 2
    shape = (others, branch.shape[0] // 2, branch.shape[1] // experts // CHUNKS)
    source_spec = pl.BlockSpec(memory_space=pltpu.HBM)
    spec = pl.BlockSpec(memory_space=pl.ANY)
    return pl.pallas_call(
        functools.partial(pack_kernel, c, flip),
        out_shape=(jax.ShapeDtypeStruct(shape, jnp.bfloat16),) * 2,
        in_specs=[smem(), source_spec],
        out_specs=(spec, spec),
        scratch_shapes=[pltpu.SemaphoreType.DMA((2 * others,))],
        compiler_params=params(),
        name="pack",
    )(position, branch)


def join_kernel(*refs):
    *part_refs, out_ref = refs
    part = part_refs[0].shape[1]
    for c, part_ref in enumerate(part_refs):
        out_ref[:, c * part : (c + 1) * part] = part_ref[...]


def spread_kernel(shares_ref, ids_ref, out_ref):
    experts, quarter, columns = shares_ref.shape
    blocks, _, features = out_ref.shape
    per_expert = blocks // experts
    for f in range(blocks):
        start = (f % per_expert) * features
        out_ref[f, :quarter] = shares_ref[f // per_expert, :, start : start + features]
        out_ref[f, quarter:] = ids_ref[...]


def sides_kernel(position_ref, *refs):
    *share_refs, own_ref, other_ref = refs
    for k, share_ref in enumerate(share_refs):
        place = position_ref[0] ^ k
        for side, out_ref in enumerate((own_ref, other_ref)):
            out_ref[:, place] = share_ref[:, position_ref[2] ^ side]


def dispatch_kernel(position_ref, ids_ref, extra_ref, *refs):
    *token_refs, out_ref = refs
    planes = len(token_refs)
    experts, _, part = out_ref.shape
    lanes = extra_ref.shape[0]
    count = out_ref.shape[1] - lanes
    capacity = count // planes
    tokens = ids_ref.shape[2]
    plane, core = position_ref[1], position_ref[2]
    slots = lax.broadcasted_iota(jnp.int32, (experts * capacity, tokens), 0)
    for k in range(planes):
        source = plane ^ k
        ids = ids_ref[source * 2 + core]
        code0 = ids[0:1] * capacity + ids[2:3]
        code1 = ids[1:2] * capacity + ids[3:4]
        one_hot = jnp.where((code0 == slots) | (code1 == slots), 1.0, 0.0).astype(jnp.bfloat16)
        picked = jnp.dot(one_hot, token_refs[k][...], preferred_element_type=jnp.float32)
        rows = pl.ds(pl.multiple_of(source * capacity, 16), capacity)
        out_ref[:, rows] = picked.reshape(experts, capacity, part).astype(jnp.bfloat16)
    for e in range(experts):
        out_ref[e, count:] = extra_ref[...]


def row_stats(flat_ref, side, aux_ref):
    count = flat_ref.shape[0] // 2
    experts, lanes, part = aux_ref.shape
    squares = jnp.zeros((count, part), jnp.float32)
    logits = jnp.zeros((count, lanes), jnp.float32)
    for e in range(experts):
        rows = flat_ref[side * count : (side + 1) * count, e * part : (e + 1) * part]
        aux = aux_ref[e]
        ratio = rows.astype(jnp.float32) * (1.0 / aux[0:1].astype(jnp.float32))
        squares = squares + ratio * ratio
        logits = logits + lax.dot_general(
            rows, aux, (((1,), (1,)), ((), ())), preferred_element_type=jnp.float32
        )
    total = jnp.sum(squares, axis=1, keepdims=True)
    return jnp.where(lax.broadcasted_iota(jnp.int32, logits.shape, 1) == 0, total, logits)


def row_copies(sides, flat_ref, aux_ref, sems):
    count = flat_ref.shape[0] // 2
    experts, _, part = aux_ref.shape
    copies = [
        pltpu.make_async_copy(sides[0].at[:, pl.ds(count, aux_ref.shape[1])], aux_ref, sems.at[0])
    ]
    for side, rows_ref in enumerate(sides):
        for e in range(experts):
            copies.append(
                pltpu.make_async_copy(
                    rows_ref.at[e, pl.ds(0, count)],
                    flat_ref.at[pl.ds(side * count, count), pl.ds(e * part, part)],
                    sems.at[1 + side * experts + e],
                )
            )
    return copies


def turned(flat_ref, e, part):
    return flat_ref[:, e * part : (e + 1) * part].T


def product(flat_ref, weight_ref):
    weight = weight_ref[...].reshape(flat_ref.shape[1], weight_ref.shape[3])
    return jnp.dot(flat_ref[...], weight, preferred_element_type=jnp.float32)


def shares_of(experts, tiles, t):
    return range(t * experts // tiles, (t + 1) * experts // tiles)


def early_kernel(
    tiles,
    own_ref,
    other_ref,
    gate_ref,
    up_ref,
    gate_out,
    up_out,
    stats_out,
    turned_out,
    flat_scratch,
    aux_scratch,
    sems,
):
    count = flat_scratch.shape[0] // 2
    experts, _, part = aux_scratch.shape

    for t in range(tiles):

        @pl.when(pl.program_id(0) == t)
        def _():
            if t == 0:
                copies = row_copies((own_ref, other_ref), flat_scratch, aux_scratch, sems)
                for copy in copies:
                    copy.start()
                for copy in copies:
                    copy.wait()
            gate_out[...] = product(flat_scratch, gate_ref)
            up_out[...] = product(flat_scratch, up_ref)
            for e in shares_of(experts, tiles, t):
                turned_out[e] = turned(flat_scratch, e, part)
            if t == tiles - 1:
                for side in range(2):
                    stats_out[side * count : (side + 1) * count] = row_stats(
                        flat_scratch, side, aux_scratch
                    )


def late_kernel(
    width,
    tiles,
    position_ref,
    own_ref,
    other_ref,
    turned_ref,
    gate_ref,
    up_ref,
    gate_acc,
    up_acc,
    stats_ref,
    signs_ref,
    cot_ref,
    hidden_out,
    grad_gate_out,
    grad_up_out,
    flat_scratch,
    aux_scratch,
    scale_scratch,
    weight_scratch,
    gate_scratch,
    up_scratch,
    d_gate_scratch,
    d_up_scratch,
    turned_scratch,
    sems,
):
    step = pl.program_id(0)
    core = position_ref[2]
    planes, _, capacity, tile = hidden_out.shape
    count = planes * capacity
    experts, _, part = aux_scratch.shape
    lanes = stats_ref.shape[1]
    turn_copy = pltpu.make_async_copy(
        turned_ref, turned_scratch.at[:, pl.ds(0, part)], sems.at[1 + 2 * experts]
    )

    def scales():
        for side in range(2):
            span = slice(side * count, (side + 1) * count)
            stats = stats_ref[span] + row_stats(flat_scratch, side, aux_scratch)
            inverse = lax.rsqrt(stats[:, 0:1] / width + 1e-05)
            signs = signs_ref[:, pl.ds(core ^ side, 1)].reshape(count, lanes)
            filled = signs[:, lanes - 1 :]
            column = lax.broadcasted_iota(jnp.int32, stats.shape, 1)
            router = (column >= 1) & (column <= experts)
            margin = jnp.sum(jnp.where(router, stats * signs, 0.0), axis=1, keepdims=True)
            prob = jax.nn.sigmoid(margin * inverse).astype(jnp.bfloat16).astype(jnp.float32)
            scale_scratch[span] = inverse
            weight_scratch[span] = jnp.where(filled > 0.0, prob, 0.0)

    def units_of(t):
        for side in range(2):
            span = slice(side * count, (side + 1) * count)
            inverse = scale_scratch[span]
            weight = weight_scratch[span]
            gate_pre = inverse * gate_scratch[t % 2, span]
            up_pre = inverse * up_scratch[t % 2, span]
            sig_gate = jax.nn.sigmoid(gate_pre)
            act_gate = gate_pre * sig_gate
            hidden = (weight * act_gate * up_pre).astype(jnp.bfloat16)
            hidden_out[:, pl.ds(core ^ side, 1)] = hidden.reshape(planes, 1, capacity, tile)
            cot = cot_ref[:, pl.ds(core ^ side, 1)].reshape(count, tile)
            d_pre = cot.astype(jnp.float32) * (weight * inverse)
            d_gate = d_pre * up_pre * sig_gate * (1.0 + gate_pre * (1.0 - sig_gate))
            columns = slice(t * tile, (t + 1) * tile)
            d_gate_scratch[span, columns] = d_gate.astype(jnp.bfloat16)
            d_up_scratch[span, columns] = (d_pre * act_gate).astype(jnp.bfloat16)

    def gradients(stretch):
        e = (step - tiles) % experts
        stretch_units = grad_gate_out.shape[2]
        span = slice(stretch * stretch_units, (stretch + 1) * stretch_units)
        for scratch, out in ((d_gate_scratch, grad_gate_out), (d_up_scratch, grad_up_out)):
            out[0] = jnp.dot(
                turned_scratch[e], scratch[:, span], preferred_element_type=jnp.float32
            ).astype(jnp.bfloat16)

    for t in range(tiles):

        @pl.when(step == t)
        def _():
            if t == 0:
                copies = row_copies((own_ref, other_ref), flat_scratch, aux_scratch, sems)
                for copy in copies:
                    copy.start()
                turn_copy.start()
                for copy in copies:
                    copy.wait()
            gate_scratch[t % 2] = gate_acc[...] + product(flat_scratch, gate_ref)
            up_scratch[t % 2] = up_acc[...] + product(flat_scratch, up_ref)
            for e in shares_of(experts, tiles, t):
                turned_scratch[e, part:] = turned(flat_scratch, e, part)
            if t == 0:
                scales()
            else:
                units_of(t - 1)

    @pl.when(step == tiles)
    def _():
        turn_copy.wait()
        units_of(tiles - 1)
        gradients(0)

    for stretch in range(tiles * tile // grad_gate_out.shape[2]):
        first = tiles + stretch * experts

        @pl.when((step >= first) & (step < first + experts) & (step > tiles))
        def _():
            gradients(stretch)


def per_device(
    branch_wo,
    context,
    residual,
    norm_gain,
    router_w,
    gate_w,
    up_w,
    expert_ids,
    slot_ids,
    cot_hidden,
):
    experts = lax.axis_size("expert")
    blocks = lax.axis_size("fsdp")
    planes = blocks // 2
    expert = lax.axis_index("expert")
    block = lax.axis_index("fsdp")
    plane, core = block // 2, block % 2
    tokens, columns = context.shape
    width = columns * experts
    features = width // blocks
    capacity = cot_hidden.shape[1] // blocks
    units = cot_hidden.shape[2]
    part = columns // CHUNKS
    quarter = tokens // experts
    count = planes * capacity
    position = jnp.stack([expert, plane, core]).astype(jnp.int32)
    bits = bits_of(experts)

    lanes = experts + 2 + (-(experts + 2)) % 16
    extra = jnp.concatenate([norm_gain[None], router_w.T])
    extra = jnp.pad(extra, ((0, lanes - extra.shape[0]), (0, 0)))
    ids = jnp.concatenate([expert_ids, slot_ids], axis=1).T.astype(jnp.bfloat16)
    id_rows = ids.size // features
    ids = jnp.pad(ids.reshape(id_rows, features), ((0, -id_rows % 16), (0, 0)))

    branch = branch_wo[0]
    weights = [1 << (bits - 1 - i) for i in range(bits)]
    own_bits = [(expert // weight) % 2 for weight in weights]

    def start_sum(kept, first):
        def value(chosen):
            place = 0
            for i in range(bits):
                place = place if i == first else 2 * place + chosen[i]
            return pick(kept, place, 0).astype(jnp.float32)

        return value

    def joined(value, got, axis, rest):
        def total(chosen):
            chosen = [own_bits[axis] if i == axis else bit for i, bit in enumerate(chosen)]
            place = 0
            for i in rest:
                place = 2 * place + chosen[i]
            return value(chosen) + pick(got, place, 0).astype(jnp.float32)

        return total

    orders = (list(range(bits))[::-1], list(range(bits)))
    held = {}

    def keep(c, position):
        for h, kept in enumerate(pack(position, branch, c, 0, experts)):
            held[c, h] = start_sum(kept, orders[h][0])

    def branch_sends(phase, c):
        if phase == 0:
            return pack(position, branch, c, 1, experts)
        sends = []
        for h, order in enumerate(orders):
            rest = sorted(order[phase + 1 :])
            stacked = []
            for code in range(1 << len(rest)):
                chosen = list(own_bits)
                chosen[order[phase]] = 1 - own_bits[order[phase]]
                for at, i in enumerate(rest):
                    chosen[i] = (code >> (len(rest) - 1 - at)) & 1
                stacked.append(held[c, h](chosen).astype(jnp.bfloat16))
            sends.append(stacked[0][None] if len(stacked) == 1 else jnp.stack(stacked))
        return tuple(sends)

    def branch_exchange(phase, sends):
        return tuple(
            exchange(sends[h], "expert", weights[order[phase]]) for h, order in enumerate(orders)
        )

    def branch_add(phase, c, got):
        for h, order in enumerate(orders):
            held[c, h] = joined(held[c, h], got[h], order[phase], sorted(order[phase + 1 :]))

    def merged_of(c):
        total = jnp.concatenate([held[c, 0](own_bits), held[c, 1](own_bits)])
        return (total / experts).astype(jnp.bfloat16)

    shares = lax.all_to_all(
        context.reshape(experts, quarter, columns), "expert", split_axis=0, concat_axis=0, tiled=True
    )

    spread_shape = (blocks, quarter + ids.shape[0], features)
    to_blocks = pl.pallas_call(
        spread_kernel,
        out_shape=jax.ShapeDtypeStruct(spread_shape, jnp.bfloat16),
        in_specs=[whole(shares.shape), whole(ids.shape)],
        out_specs=whole(spread_shape),
        grid=(1,),
        compiler_params=params(),
        name="spread",
    )(shares, ids)
    got = branch_exchange(0, pack(after(position, shares), branch, 0, 1, experts))
    keep(0, after(position, to_blocks))
    branch_add(0, 0, after(got, to_blocks))
    from_blocks = lax.all_to_all(to_blocks, "fsdp", split_axis=0, concat_axis=0, tiled=True)
    for phase in range(1, bits):
        got = branch_exchange(phase, branch_sends(phase, 0))
        if phase == bits - 1:
            from_blocks, got = lax.optimization_barrier((from_blocks, got))
        branch_add(phase, 0, got)

    ids_all = from_blocks[:, quarter : quarter + id_rows].astype(jnp.int32)
    ids_all = ids_all.reshape(blocks, 4, tokens)
    own_share = from_blocks[:, :quarter]
    packed1 = branch_sends(0, 1)
    keep(1, after(position, packed1))
    pieces = [exchange(own_share, "expert", k) if k else own_share for k in range(experts)]
    pieces, packed1 = lax.optimization_barrier((pieces, packed1))
    side_shape = (planes, experts, quarter, features)
    sides = pl.pallas_call(
        sides_kernel,
        out_shape=(jax.ShapeDtypeStruct(side_shape, jnp.bfloat16),) * 2,
        in_specs=[smem()] + [whole((planes, 2, quarter, features))] * experts,
        out_specs=(whole(side_shape),) * 2,
        grid=(1,),
        compiler_params=params(),
        name="sides",
    )(position, *[piece.reshape(planes, 2, quarter, features) for piece in pieces])
    sides = [side.reshape(planes * tokens, features) for side in sides]
    signs = pl.pallas_call(
        functools.partial(signs_kernel, experts),
        out_shape=jax.ShapeDtypeStruct((blocks, capacity, lanes), jnp.float32),
        in_specs=[smem(), whole(ids_all.shape)],
        out_specs=whole((blocks, capacity, lanes)),
        grid=(1,),
        compiler_params=params(),
        name="signs",
    )(position, ids_all).reshape(planes, 2, capacity, lanes)

    gate_view = gate_w.reshape(experts, CHUNKS, part, units)
    up_view = up_w.reshape(experts, CHUNKS, part, units)
    tile = min(256, units)
    stretch = min(512, units)
    tiles = units // tile
    def pair_of(merged):
        def attend(rows):
            out = jnp.dot(rows, merged, preferred_element_type=jnp.float32)
            return out.reshape(planes, tokens, part)

        swapped = exchange(attend(sides[1]).astype(jnp.bfloat16), "fsdp", 1)
        return attend(sides[0]) + swapped.astype(jnp.float32)

    def plane_sends(pair):
        return [pick(pair, plane ^ k, 0).astype(jnp.bfloat16) for k in range(1, planes)]

    def plane_exchange(sends):
        return [exchange(send, "fsdp", 2 * k) for k, send in enumerate(sends, 1)]

    def scaled_of(c, pair, arrived):
        span = slice(c * part, (c + 1) * part)
        hstate = residual[:, span].astype(jnp.float32) + pick(pair, plane, 0)
        for value in arrived:
            hstate = hstate + value.astype(jnp.float32)
        return (hstate * norm_gain[span].astype(jnp.float32)).astype(jnp.bfloat16)

    height = count + lanes

    def slots_of(c, own_tokens):
        return pl.pallas_call(
            dispatch_kernel,
            out_shape=jax.ShapeDtypeStruct((experts, height, part), jnp.bfloat16),
            in_specs=[smem(), whole(ids_all.shape)]
            + [pl.BlockSpec((lanes, part), lambda i, c=c: (0, c))]
            + [whole((tokens, part))] * planes,
            out_specs=whole((experts, height, part)),
            grid=(1,),
            compiler_params=params(),
            name="dispatch",
        )(position, ids_all, extra, *own_tokens)

    merged0 = merged_of(0)
    got = branch_exchange(0, packed1)
    pair0 = pair_of(merged0)
    sends0 = plane_sends(pair0)
    branch_add(0, 1, after(got, sends0))
    arrived0 = plane_exchange(sends0)
    for phase in range(1, bits):
        got = branch_exchange(phase, branch_sends(phase, 1))
        if phase < bits - 1:
            branch_add(phase, 1, got)

    scaled0 = scaled_of(0, pair0, arrived0)
    tokens0 = [scaled0] + plane_exchange([scaled0] * (planes - 1))
    if bits > 1:
        branch_add(bits - 1, 1, after(got, scaled0))
    merged1 = merged_of(1)
    merged_out = pl.pallas_call(
        join_kernel,
        out_shape=jax.ShapeDtypeStruct((features, columns), jnp.bfloat16),
        in_specs=[whole((features, part))] * CHUNKS,
        out_specs=whole((features, columns)),
        grid=(1,),
        compiler_params=params(),
        name="join",
    )(merged0, merged1)
    pair1 = pair_of(merged1)
    sends1 = plane_sends(pair1)
    arrived1 = plane_exchange(sends1)

    scaled1 = scaled_of(1, pair1, arrived1)
    slots0 = slots_of(0, after(tokens0, scaled1))
    tokens1 = [scaled1] + plane_exchange([scaled1] * (planes - 1))
    slots1 = slots_of(1, tokens1)
    slots = (slots0, slots1)

    def to_experts(c):
        return lax.all_to_all(slots[c], "expert", split_axis=0, concat_axis=0, tiled=True)

    rows = after(to_experts(0), slots[-1], merged_out, signs)
    other = exchange(rows, "fsdp", 1)
    weight_spec = pl.BlockSpec((experts, 1, part, tile), lambda n: (0, 0, 0, n))
    sums = jax.ShapeDtypeStruct((2 * count, units), jnp.float32)
    sum_spec = pl.BlockSpec((2 * count, tile), lambda n: (0, n))
    any_spec = pl.BlockSpec(memory_space=pl.ANY)
    row_scratch = [
        pltpu.VMEM((2 * count, experts * part), jnp.bfloat16),
        pltpu.VMEM((experts, lanes, part), jnp.bfloat16),
    ]
    partial = pl.pallas_call(
        functools.partial(early_kernel, tiles),
        out_shape=(
            sums,
            sums,
            jax.ShapeDtypeStruct((2 * count, lanes), jnp.float32),
            jax.ShapeDtypeStruct((experts, part, 2 * count), jnp.bfloat16),
        ),
        in_specs=[any_spec, any_spec, weight_spec, weight_spec],
        out_specs=(
            sum_spec,
            sum_spec,
            whole((2 * count, lanes)),
            whole((experts, part, 2 * count)),
        ),
        grid=(tiles,),
        scratch_shapes=row_scratch + [pltpu.SemaphoreType.DMA((1 + 2 * experts,))],
        compiler_params=params(60),
        cost_estimate=pl.CostEstimate(
            flops=8 * count * experts * part * units,
            bytes_accessed=4 * experts * part * units,
            transcendentals=0,
        ),
        name="early",
    )(rows, other, gate_view, up_view)
    rows = after(to_experts(1), partial)
    other = exchange(rows, "fsdp", 1)

    tile_of = lambda i: jnp.minimum(i, tiles - 1)
    behind = lambda i: jnp.clip(i - 1, 0, tiles - 1)
    place_of = lambda i: jnp.maximum(i - tiles, 0)
    weight_spec = pl.BlockSpec((experts, 1, part, tile), lambda i: (0, 1, 0, tile_of(i)))
    sum_spec = pl.BlockSpec((2 * count, tile), lambda i: (0, tile_of(i)))
    unit_spec = pl.BlockSpec((planes, 2, capacity, tile), lambda i: (0, 0, 0, behind(i)))
    grad_spec = pl.BlockSpec(
        (1, columns, stretch), lambda i: (place_of(i) % experts, 0, place_of(i) // experts)
    )
    grad_shape = jax.ShapeDtypeStruct((experts, columns, units), jnp.bfloat16)
    gate_sums, up_sums, stats, turned_rows = partial
    hidden, grad_gate, grad_up = pl.pallas_call(
        functools.partial(late_kernel, float(width), tiles),
        out_shape=(
            jax.ShapeDtypeStruct((planes, 2, capacity, units), jnp.bfloat16),
            grad_shape,
            grad_shape,
        ),
        in_specs=[smem(), any_spec, any_spec, any_spec]
        + [weight_spec, weight_spec, sum_spec, sum_spec]
        + [whole(stats.shape), whole(signs.shape), unit_spec],
        out_specs=(unit_spec, grad_spec, grad_spec),
        grid=(tiles + experts * (units // stretch),),
        scratch_shapes=row_scratch
        + [
            pltpu.VMEM((2 * count, 1), jnp.float32),
            pltpu.VMEM((2 * count, 1), jnp.float32),
            pltpu.VMEM((2, 2 * count, tile), jnp.float32),
            pltpu.VMEM((2, 2 * count, tile), jnp.float32),
            pltpu.VMEM((2 * count, units), jnp.bfloat16),
            pltpu.VMEM((2 * count, units), jnp.bfloat16),
            pltpu.VMEM((experts, columns, 2 * count), jnp.bfloat16),
            pltpu.SemaphoreType.DMA((2 + 2 * experts,)),
        ],
        compiler_params=params(60),
        name="late",
    )(
        position,
        rows,
        other,
        turned_rows,
        gate_view,
        up_view,
        gate_sums,
        up_sums,
        stats,
        signs,
        cot_hidden.reshape(planes, 2, capacity, units),
    )
    return (
        merged_out,
        hidden.reshape(1, -1, units),
        grad_gate.reshape(1, width, units),
        grad_up.reshape(1, width, units),
    )


def solution(mesh):
    placed = (
        P("expert", "fsdp", None),
        P("fsdp", "expert"),
        P("fsdp", "expert"),
        P("expert"),
        P("expert", None),
        P("expert", None, "fsdp"),
        P("expert", None, "fsdp"),
        P("fsdp", None),
        P("fsdp", None),
        P("expert", None, "fsdp"),
    )
    return jax.shard_map(
        per_device,
        mesh=mesh,
        in_specs=placed,
        out_specs=(
            P("fsdp", "expert"),
            P("expert", None, "fsdp"),
            P("expert", None, "fsdp"),
            P("expert", None, "fsdp"),
        ),
        check_vma=False,
    )
```

profile of v0, /device:TPU:0, one launch (start us, length us, event | category | flops | bytes accessed | tf_op | source)
XLA Modules:
  0.0 198.2 jit_solution(11084610731244095357)
XLA Ops:
  0.7 5.3 %all-to-all-start = ((bf16[4,32,1024]{2,1,0:T(8,128)(2,1)}), bf16[4,32,1024]{2,1,0:T(8,128)(2,1)S(1)}, u32[]{:S(2)}, u32[]{:S(2)}) async-start(bf16[4,32,1024]{2,1,0:T(8,128)(2,1)} %bitcast.110), calls=%async_computation | async-start | bytes 524288 | tf_op jit(solution)/shard_map/all_to_all | solution.py:441
  6.0 5.3 %all-to-all-done.shares_ref = bf16[4,32,1024]{2,1,0:T(8,128)(2,1)S(1)} async-done(((bf16[4,32,1024]{2,1,0:T(8,128)(2,1)}), bf16[4,32,1024]{2,1,0:T(8,128)(2,1)S(1)}, u32[]{:S(2)}, u32[]{:S(2)}) %all-to-all-start) | async-done | bytes 262176 | tf_op jit(solution)/shard_map/all_to_all | solution.py:441
  11.3 2.2 %copy-done = bf16[1,512,4096]{2,1,0:T(8,128)(2,1)S(1)} copy-done((bf16[1,512,4096]{2,1,0:T(8,128)(2,1)S(1)}, bf16[1,512,4096]{2,1,0:T(8,128)(2,1)}, u32[]{:S(2)}) %copy-start) | copy-done | bytes 4194328
  14.2 1.3 collective-permute-start
  16.2 0.8 spread.1
  16.9 4.9 %all-to-all-start.1 = ((bf16[8,48,512]{2,1,0:T(8,128)(2,1)}), bf16[8,48,512]{2,1,0:T(8,128)(2,1)S(1)}, u32[]{:S(2)}, u32[]{:S(2)}) async-start(bf16[8,48,512]{2,1,0:T(8,128)(2,1)} %spread.1), calls=%async_computation.1 | async-start | bytes 786432 | tf_op jit(solution)/shard_map/all_to_all | solution.py:458
  21.8 2.2 %copy-done.1 = bf16[1,512,4096]{2,1,0:T(8,128)(2,1)S(1)} copy-done((bf16[1,512,4096]{2,1,0:T(8,128)(2,1)S(1)}, bf16[1,512,4096]{2,1,0:T(8,128)(2,1)}, u32[]{:S(2)}) %copy-start.1) | copy-done | bytes 4194328
  24.7 1.8 collective-permute-done
  26.5 1.1 collective-permute-done.1
  27.6 1.7 add_convert_fusion.2
  29.3 0.8 collective-permute-start.3
  30.9 1.5 collective-permute-start.2
  32.4 2.2 %copy-done.2 = bf16[1,512,4096]{2,1,0:T(8,128)(2,1)S(1)} copy-done((bf16[1,512,4096]{2,1,0:T(8,128)(2,1)S(1)}, bf16[1,512,4096]{2,1,0:T(8,128)(2,1)}, u32[]{:S(2)}) %copy-start.2) | copy-done | bytes 4194328
  34.5 1.4 pack.6
  36.0 1.5 collective-permute-done.2
  37.5 1.4 collective-permute-start.6
  38.9 1.4 collective-permute-start.5
  40.3 0.8 collective-permute-start.4
  41.0 1.3 add_bitcast_fusion.2
  42.5 4.3 %collective-permute-done.6 = bf16[8,32,512]{2,1,0:T(8,128)(2,1)S(1)} collective-permute-done((bf16[8,32,512]{2,1,0:T(8,128)(2,1)S(1)}, bf16[8,32,512]{2,1,0:T(8,128)(2,1)S(1)}, u32[]{:S(2)}, u32[]{:S(2)}) %collective-permute-start.6) | collective-permute-done | bytes 262176 | tf_op jit(solution)/shard_map/ppermute | solution.py:16
  46.8 2.7 %collective-permute-done.5 = bf16[8,32,512]{2,1,0:T(8,128)(2,1)S(1)} collective-permute-done((bf16[8,32,512]{2,1,0:T(8,128)(2,1)S(1)}, bf16[8,32,512]{2,1,0:T(8,128)(2,1)S(1)}, u32[]{:S(2)}, u32[]{:S(2)}) %collective-permute-start.5) | collective-permute-done | bytes 262176 | tf_op jit(solution)/shard_map/ppermute | solution.py:16
  50.1 1.2 convolution_convert_fusion.1
  51.3 0.9 collective-permute-start.7
  52.2 1.2 collective-permute-start.8
  53.3 2.2 %copy-done.3 = bf16[1,512,4096]{2,1,0:T(8,128)(2,1)S(1)} copy-done((bf16[1,512,4096]{2,1,0:T(8,128)(2,1)S(1)}, bf16[1,512,4096]{2,1,0:T(8,128)(2,1)}, u32[]{:S(2)}) %copy-start.3) | copy-done | bytes 4194328
  56.2 1.5 convert_add_fusion.1
  57.7 0.8 fusion.24
  58.6 3.5 %collective-permute-start.14 = (bf16[128,512]{1,0:T(8,128)(2,1)}, bf16[128,512]{1,0:T(8,128)(2,1)}, u32[]{:S(2)}, u32[]{:S(2)}) collective-permute-start(bf16[128,512]{1,0:T(8,128)(2,1)} %get-tuple-element.89), channel_id=1, source_target_pairs={{0,6},{1,7},{2,4},{3,5},{4,2},{5,3},{6,0},{7,1},{8,14},{9,15},{10,... | collective-permute-start | bytes 393224 | tf_op jit(solution)/shard_map/ppermute | solution.py:16
  62.1 0.9 collective-permute-start.12
  63.0 3.0 %collective-permute-done.7 = bf16[2,256,512]{2,1,0:T(8,128)(2,1)} collective-permute-done((bf16[2,256,512]{2,1,0:T(8,128)(2,1)}, bf16[2,256,512]{2,1,0:T(8,128)(2,1)}, u32[]{:S(2)}, u32[]{:S(2)}) %collective-permute-start.7) | collective-permute-done | bytes 524320 | tf_op jit(solution)/shard_map/ppermute | solution.py:16
  66.3 1.7 add_convert_fusion
  68.1 1.1 collective-permute-start.11
  69.2 1.7 add_convert_fusion.1
  70.9 0.9 collective-permute-start.10
  71.8 2.0 %collective-permute-done.13 = bf16[128,512]{1,0:T(8,128)(2,1)} collective-permute-done((bf16[128,512]{1,0:T(8,128)(2,1)}, bf16[128,512]{1,0:T(8,128)(2,1)}, u32[]{:S(2)}, u32[]{:S(2)}) %collective-permute-start.13) | collective-permute-done | bytes 131104 | tf_op jit(solution)/shard_map/ppermute | solution.py:16
  73.9 1.3 fusion.21.refs_0_
  75.1 0.8 collective-permute-done.11
  75.9 2.6 %collective-permute-done.10 = bf16[1,256,512]{2,1,0:T(8,128)(2,1)S(1)} collective-permute-done((bf16[1,256,512]{2,1,0:T(8,128)(2,1)}, bf16[1,256,512]{2,1,0:T(8,128)(2,1)S(1)}, u32[]{:S(2)}, u32[]{:S(2)}) %collective-permute-start.10) | collective-permute-done | bytes 262176 | tf_op jit(solution)/shard_map/ppermute | solution.py:16
  78.5 1.0 add_bitcast_fusion
  79.5 1.0 add_bitcast_fusion.1
  81.3 1.8 collective-permute-done.15
  83.6 1.7 collective-permute-start.16
  85.4 2.4 %collective-permute-start.18 = (bf16[128,512]{1,0:T(8,128)(2,1)S(1)}, bf16[128,512]{1,0:T(8,128)(2,1)S(1)}, u32[]{:S(2)}, u32[]{:S(2)}) collective-permute-start(bf16[128,512]{1,0:T(8,128)(2,1)S(1)} %get-tuple-element.87), channel_id=1, source_target_pairs={{0,6},{1,7},{2,4},{3,5},{4,2},{5,3},{6,0},{7,1},{8,14},{9,15},{10,... | collective-permute-start | bytes 393224 | tf_op jit(solution)/shard_map/ppermute | solution.py:16
  87.8 3.0 %collective-permute-start.24 = (bf16[128,512]{1,0:T(8,128)(2,1)S(1)}, bf16[128,512]{1,0:T(8,128)(2,1)S(1)}, u32[]{:S(2)}, u32[]{:S(2)}) collective-permute-start(bf16[128,512]{1,0:T(8,128)(2,1)S(1)} %fusion.21.refs_0_), channel_id=1, source_target_pairs={{0,6},{1,7},{2,4},{3,5},{4,2},{5,3},{6,0},{7,1},{8,14},{9,15},{10,... | collective-permute-start | bytes 393224 | tf_op jit(solution)/shard_map/ppermute | solution.py:16
  91.3 0.9 collective-permute-start.22
  92.2 2.8 %collective-permute-done.18 = bf16[128,512]{1,0:T(8,128)(2,1)S(1)} collective-permute-done((bf16[128,512]{1,0:T(8,128)(2,1)S(1)}, bf16[128,512]{1,0:T(8,128)(2,1)S(1)}, u32[]{:S(2)}, u32[]{:S(2)}) %collective-permute-start.18) | collective-permute-done | bytes 131104 | tf_op jit(solution)/shard_map/ppermute | solution.py:16
  95.0 10.9 %collective-permute-done.17 = bf16[128,512]{1,0:T(8,128)(2,1)S(1)} collective-permute-done((bf16[128,512]{1,0:T(8,128)(2,1)S(1)}, bf16[128,512]{1,0:T(8,128)(2,1)S(1)}, u32[]{:S(2)}, u32[]{:S(2)}) %collective-permute-start.17) | collective-permute-done | bytes 131104 | tf_op jit(solution)/shard_map/ppermute | solution.py:16
  106.0 4.9 %collective-permute-done.23.refs_2_ = bf16[128,512]{1,0:T(8,128)(2,1)S(1)} collective-permute-done((bf16[128,512]{1,0:T(8,128)(2,1)S(1)}, bf16[128,512]{1,0:T(8,128)(2,1)S(1)}, u32[]{:S(2)}, u32[]{:S(2)}) %collective-permute-start.23) | collective-permute-done | bytes 131104 | tf_op jit(solution)/shard_map/ppermute | solution.py:16
  110.9 2.3 %dispatch.3 = bf16[4,400,512]{2,1,0:T(8,128)(2,1)} custom-call(s32[3]{0:T(128)S(1)} %pad_add_fusion.position_ref, s32[8,4,128]{2,1,0:T(4,128)S(1)} %bitcast.99, bf16[16,1024]{1,0:T(8,128)(2,1)S(1)} %fusion.30.extra_ref, bf16[128,512]{1,0:T(8,128)(2,1)S(1)} %fusion.21.refs_0_, bf16[128,512]{1,0:T(8,128)(2,1)S(1)} %collective-permute-done.22.refs_1_, ...), custom_call_target="tpu_custom_call" | custom-call | tf_op jit(solution)/shard_map/dispatch/pallas_call | solution.py:522
  113.2 3.6 %all-to-all-start.3 = ((bf16[4,400,512]{2,1,0:T(8,128)(2,1)}), bf16[4,400,512]{2,1,0:T(8,128)(2,1)S(1)}, u32[]{:S(2)}, u32[]{:S(2)}) async-start(bf16[4,400,512]{2,1,0:T(8,128)(2,1)} %dispatch.3), calls=%async_computation.3 | async-start | bytes 3276800 | tf_op jit(solution)/shard_map/all_to_all | solution.py:570
  116.8 2.7 %collective-permute-start.21 = (bf16[128,512]{1,0:T(8,128)(2,1)S(1)}, bf16[128,512]{1,0:T(8,128)(2,1)S(1)}, u32[]{:S(2)}, u32[]{:S(2)}) collective-permute-start(bf16[128,512]{1,0:T(8,128)(2,1)S(1)} %fusion.16.refs_0_), channel_id=1, source_target_pairs={{0,6},{1,7},{2,4},{3,5},{4,2},{5,3},{6,0},{7,1},{8,14},{9,15},{10,... | collective-permute-start | bytes 393224 | tf_op jit(solution)/shard_map/ppermute | solution.py:16
  119.5 1.7 collective-permute-start.19
  121.2 0.8 signs.1
  122.0 1.1 join.1
  123.1 2.0 collective-permute-done.21.refs_3_
  125.1 4.4 %collective-permute-done.20.refs_2_ = bf16[128,512]{1,0:T(8,128)(2,1)S(1)} collective-permute-done((bf16[128,512]{1,0:T(8,128)(2,1)S(1)}, bf16[128,512]{1,0:T(8,128)(2,1)S(1)}, u32[]{:S(2)}, u32[]{:S(2)}) %collective-permute-start.20) | collective-permute-done | bytes 131104 | tf_op jit(solution)/shard_map/ppermute | solution.py:16
  129.5 2.3 %dispatch.2 = bf16[4,400,512]{2,1,0:T(8,128)(2,1)} custom-call(s32[3]{0:T(128)S(1)} %pad_add_fusion.position_ref, s32[8,4,128]{2,1,0:T(4,128)S(1)} %bitcast.101, bf16[16,1024]{1,0:T(8,128)(2,1)S(1)} %fusion.30.extra_ref, bf16[128,512]{1,0:T(8,128)(2,1)S(1)} %fusion.16.refs_0_, bf16[128,512]{1,0:T(8,128)(2,1)S(1)} %collective-permute-done.19.refs_1_, ...), custom_call_target="tpu_custom_call" | custom-call | tf_op jit(solution)/shard_map/dispatch/pallas_call | solution.py:522
  131.8 4.9 %all-to-all-done.3.own_ref = bf16[4,400,512]{2,1,0:T(8,128)(2,1)S(1)} async-done(((bf16[4,400,512]{2,1,0:T(8,128)(2,1)}), bf16[4,400,512]{2,1,0:T(8,128)(2,1)S(1)}, u32[]{:S(2)}, u32[]{:S(2)}) %all-to-all-start.3) | async-done | bytes 1638432 | tf_op jit(solution)/shard_map/all_to_all | solution.py:570
  136.7 3.8 %all-to-all-start.2 = ((bf16[4,400,512]{2,1,0:T(8,128)(2,1)}), bf16[4,400,512]{2,1,0:T(8,128)(2,1)S(1)}, u32[]{:S(2)}, u32[]{:S(2)}) async-start(bf16[4,400,512]{2,1,0:T(8,128)(2,1)} %dispatch.2), calls=%async_computation.2 | async-start | bytes 3276800 | tf_op jit(solution)/shard_map/all_to_all | solution.py:570
  140.5 15.0 %early.1 = (f32[768,1024]{1,0:T(8,128)}, f32[768,1024]{1,0:T(8,128)}, f32[768,16]{1,0:T(8,128)}, bf16[4,512,768]{2,1,0:T(8,128)(2,1)}) custom-call(bf16[4,400,512]{2,1,0:T(8,128)(2,1)} %copy-done.8, bf16[4,400,512]{2,1,0:T(8,128)(2,1)} %collective-permute-done.25.other_ref, bf16[4,2,512,1024]{3,2,1,0:T(8,128)(2,1)} %bitcast.105, ...), custom_call_target="tpu_custom_call" | custom-call | flops 6442450944 | bytes 8388608 | tf_op jit(solution)/shard_map/early/pallas_call | solution.py:582
  155.4 5.7 %all-to-all-done.2.own_ref = bf16[4,400,512]{2,1,0:T(8,128)(2,1)S(1)} async-done(((bf16[4,400,512]{2,1,0:T(8,128)(2,1)}), bf16[4,400,512]{2,1,0:T(8,128)(2,1)S(1)}, u32[]{:S(2)}, u32[]{:S(2)}) %all-to-all-start.2) | async-done | bytes 1638432 | tf_op jit(solution)/shard_map/all_to_all | solution.py:570
  161.1 3.5 %collective-permute-done.26.other_ref = bf16[4,400,512]{2,1,0:T(8,128)(2,1)S(1)} collective-permute-done((bf16[4,400,512]{2,1,0:T(8,128)(2,1)S(1)}, bf16[4,400,512]{2,1,0:T(8,128)(2,1)S(1)}, u32[]{:S(2)}, u32[]{:S(2)}) %collective-permute-start.26) | collective-permute-done | bytes 1638432 | tf_op jit(solution)/shard_map/ppermute | solution.py:16
  164.6 1.2 copy-done.9
  165.9 32.1 %late.1 = (bf16[4,2,96,1024]{3,2,1,0:T(8,128)(2,1)}, bf16[4,1024,1024]{2,1,0:T(8,128)(2,1)}, bf16[4,1024,1024]{2,1,0:T(8,128)(2,1)}) custom-call(s32[3]{0:T(128)} %copy-done.5, bf16[4,400,512]{2,1,0:T(8,128)(2,1)} %copy-done.6, bf16[4,400,512]{2,1,0:T(8,128)(2,1)} %copy-done.9, bf16[4,512,768]{2,1,0:T(8,128)(2,1)} %get-tuple-element.81.turned_ref, ...), custom_call_target="tpu_custom_call" | custom-call | tf_op jit(solution)/shard_map/late/pallas_call | solution.py:621
  (72 shorter events, 6.6 us)
Async XLA Ops:
  0.6 15.5 %copy-start.15 = (s32[128,2]{0,1:T(2,128)S(1)}, s32[128,2]{0,1:T(2,128)}, u32[]{:S(2)}) copy-start(s32[128,2]{0,1:T(2,128)} %param.17) | copy-start | bytes 3076
  0.6 15.5 %copy-start.16 = (s32[128,2]{0,1:T(2,128)S(1)}, s32[128,2]{0,1:T(2,128)}, u32[]{:S(2)}) copy-start(s32[128,2]{0,1:T(2,128)} %param.18) | copy-start | bytes 3076
  0.7 10.7 %all-to-all-start = ((bf16[4,32,1024]{2,1,0:T(8,128)(2,1)}), bf16[4,32,1024]{2,1,0:T(8,128)(2,1)S(1)}, u32[]{:S(2)}, u32[]{:S(2)}) async-start(bf16[4,32,1024]{2,1,0:T(8,128)(2,1)} %bitcast.110), calls=%async_computation | async-start | bytes 524288 | tf_op jit(solution)/shard_map/all_to_all | solution.py:441
  6.0 123.5 %copy-start.5 = (s32[3]{0:T(128)}, s32[3]{0:T(128)S(1)}, u32[]{:S(2)}) copy-start(s32[3]{0:T(128)S(1)} %pad_add_fusion.position_ref) | copy-start | bytes 40
  11.3 2.2 %copy-start = (bf16[1,512,4096]{2,1,0:T(8,128)(2,1)S(1)}, bf16[1,512,4096]{2,1,0:T(8,128)(2,1)}, u32[]{:S(2)}) copy-start(bf16[1,512,4096]{2,1,0:T(8,128)(2,1)} %param.10) | copy-start | bytes 12582916
  14.2 12.3 %collective-permute-start = (bf16[2,256,512]{2,1,0:T(8,128)(2,1)S(1)}, bf16[2,256,512]{2,1,0:T(8,128)(2,1)S(1)}, u32[]{:S(2)}, u32[]{:S(2)}) collective-permute-start(bf16[2,256,512]{2,1,0:T(8,128)(2,1)S(1)} %get-tuple-element.48), channel_id=1, source_target_pairs={{0,8},{8,0},{16,24},{24,16},{1,9},{9,1},{17,25},{25,17},{2,10},{10... | collective-permute-start | bytes 1572872 | tf_op jit(solution)/shard_map/ppermute | solution.py:16
  15.5 12.1 %collective-permute-start.1 = (bf16[2,256,512]{2,1,0:T(8,128)(2,1)S(1)}, bf16[2,256,512]{2,1,0:T(8,128)(2,1)}, u32[]{:S(2)}, u32[]{:S(2)}) collective-permute-start(bf16[2,256,512]{2,1,0:T(8,128)(2,1)S(1)} %get-tuple-element.49), channel_id=1, source_target_pairs={{0,16},{8,24},{16,0},{24,8},{1,17},{9,25},{17,1},{25,9},{2,18},{10... | collective-permute-start | bytes 1572872 | tf_op jit(solution)/shard_map/ppermute | solution.py:16
  16.9 19.0 %all-to-all-start.1 = ((bf16[8,48,512]{2,1,0:T(8,128)(2,1)}), bf16[8,48,512]{2,1,0:T(8,128)(2,1)S(1)}, u32[]{:S(2)}, u32[]{:S(2)}) async-start(bf16[8,48,512]{2,1,0:T(8,128)(2,1)} %spread.1), calls=%async_computation.1 | async-start | bytes 786432 | tf_op jit(solution)/shard_map/all_to_all | solution.py:458
  21.8 2.2 %copy-start.1 = (bf16[1,512,4096]{2,1,0:T(8,128)(2,1)S(1)}, bf16[1,512,4096]{2,1,0:T(8,128)(2,1)}, u32[]{:S(2)}) copy-start(bf16[1,512,4096]{2,1,0:T(8,128)(2,1)} %param.10) | copy-start | bytes 12582916
  29.3 6.6 %collective-permute-start.3 = (bf16[1,256,512]{2,1,0:T(8,128)(2,1)}, bf16[1,256,512]{2,1,0:T(8,128)(2,1)S(1)}, u32[]{:S(2)}, u32[]{:S(2)}) collective-permute-start(bf16[1,256,512]{2,1,0:T(8,128)(2,1)} %add_convert_fusion.2), channel_id=1, source_target_pairs={{0,8},{8,0},{16,24},{24,16},{1,9},{9,1},{17,25},{25,17},{2,10},{10... | collective-permute-start | bytes 786440 | tf_op jit(solution)/shard_map/ppermute | solution.py:16
  30.9 6.6 %collective-permute-start.2 = (bf16[1,256,512]{2,1,0:T(8,128)(2,1)}, bf16[1,256,512]{2,1,0:T(8,128)(2,1)S(1)}, u32[]{:S(2)}, u32[]{:S(2)}) collective-permute-start(bf16[1,256,512]{2,1,0:T(8,128)(2,1)} %add_convert_fusion.3), channel_id=1, source_target_pairs={{0,16},{8,24},{16,0},{24,8},{1,17},{9,25},{17,1},{25,9},{2,18},{10... | collective-permute-start | bytes 786440 | tf_op jit(solution)/shard_map/ppermute | solution.py:16
  32.4 2.2 %copy-start.2 = (bf16[1,512,4096]{2,1,0:T(8,128)(2,1)S(1)}, bf16[1,512,4096]{2,1,0:T(8,128)(2,1)}, u32[]{:S(2)}) copy-start(bf16[1,512,4096]{2,1,0:T(8,128)(2,1)} %param.10) | copy-start | bytes 12582916
  36.0 4.3 %copy-start.11 = (bf16[1,256,512]{2,1,0:T(8,128)(2,1)}, bf16[1,256,512]{2,1,0:T(8,128)(2,1)S(1)}, u32[]{:S(2)}) copy-start(bf16[1,256,512]{2,1,0:T(8,128)(2,1)S(1)} %collective-permute-done.3) | copy-start | bytes 786436
  37.4 2.8 %copy-start.12 = (bf16[1,256,512]{2,1,0:T(8,128)(2,1)}, bf16[1,256,512]{2,1,0:T(8,128)(2,1)S(1)}, u32[]{:S(2)}) copy-start(bf16[1,256,512]{2,1,0:T(8,128)(2,1)S(1)} %collective-permute-done.2) | copy-start | bytes 786436
  37.5 9.3 %collective-permute-start.6 = (bf16[8,32,512]{2,1,0:T(8,128)(2,1)S(1)}, bf16[8,32,512]{2,1,0:T(8,128)(2,1)S(1)}, u32[]{:S(2)}, u32[]{:S(2)}) collective-permute-start(bf16[8,32,512]{2,1,0:T(8,128)(2,1)S(1)} %slice.18), channel_id=1, source_target_pairs={{0,24},{8,16},{16,8},{24,0},{1,25},{9,17},{17,9},{25,1},{2,26},{10... | collective-permute-start | bytes 786440 | tf_op jit(solution)/shard_map/ppermute | solution.py:16
  38.9 10.6 %collective-permute-start.5 = (bf16[8,32,512]{2,1,0:T(8,128)(2,1)S(1)}, bf16[8,32,512]{2,1,0:T(8,128)(2,1)S(1)}, u32[]{:S(2)}, u32[]{:S(2)}) collective-permute-start(bf16[8,32,512]{2,1,0:T(8,128)(2,1)S(1)} %slice.18), channel_id=1, source_target_pairs={{0,16},{8,24},{16,0},{24,8},{1,17},{9,25},{17,1},{25,9},{2,18},{10... | collective-permute-start | bytes 786440 | tf_op jit(solution)/shard_map/ppermute | solution.py:16
  40.3 9.2 %collective-permute-start.4 = (bf16[8,32,512]{2,1,0:T(8,128)(2,1)S(1)}, bf16[8,32,512]{2,1,0:T(8,128)(2,1)S(1)}, u32[]{:S(2)}, u32[]{:S(2)}) collective-permute-start(bf16[8,32,512]{2,1,0:T(8,128)(2,1)S(1)} %slice.18), channel_id=1, source_target_pairs={{0,8},{8,0},{16,24},{24,16},{1,9},{9,1},{17,25},{25,17},{2,10},{10... | collective-permute-start | bytes 786440 | tf_op jit(solution)/shard_map/ppermute | solution.py:16
  51.3 4.9 %collective-permute-start.9 = (bf16[4,128,512]{2,1,0:T(8,128)(2,1)}, bf16[4,128,512]{2,1,0:T(8,128)(2,1)}, u32[]{:S(2)}, u32[]{:S(2)}) collective-permute-start(bf16[4,128,512]{2,1,0:T(8,128)(2,1)} %convolution_convert_fusion.1), channel_id=1, source_target_pairs={{0,1},{1,0},{2,3},{3,2},{4,5},{5,4},{6,7},{7,6},{8,9},{9,8},{10,11... | collective-permute-start | bytes 1572872 | tf_op jit(solution)/shard_map/ppermute | solution.py:16
  51.3 14.7 %collective-permute-start.7 = (bf16[2,256,512]{2,1,0:T(8,128)(2,1)}, bf16[2,256,512]{2,1,0:T(8,128)(2,1)}, u32[]{:S(2)}, u32[]{:S(2)}) collective-permute-start(bf16[2,256,512]{2,1,0:T(8,128)(2,1)} %get-tuple-element.60), channel_id=1, source_target_pairs={{0,8},{8,0},{16,24},{24,16},{1,9},{9,1},{17,25},{25,17},{2,10},{10... | collective-permute-start | bytes 1572872 | tf_op jit(solution)/shard_map/ppermute | solution.py:16
  52.2 14.2 %collective-permute-start.8 = (bf16[2,256,512]{2,1,0:T(8,128)(2,1)S(1)}, bf16[2,256,512]{2,1,0:T(8,128)(2,1)}, u32[]{:S(2)}, u32[]{:S(2)}) collective-permute-start(bf16[2,256,512]{2,1,0:T(8,128)(2,1)S(1)} %get-tuple-element.61), channel_id=1, source_target_pairs={{0,16},{8,24},{16,0},{24,8},{1,17},{9,25},{17,1},{25,9},{2,18},{10... | collective-permute-start | bytes 1572872 | tf_op jit(solution)/shard_map/ppermute | solution.py:16
  53.3 2.2 %copy-start.3 = (bf16[1,512,4096]{2,1,0:T(8,128)(2,1)S(1)}, bf16[1,512,4096]{2,1,0:T(8,128)(2,1)}, u32[]{:S(2)}) copy-start(bf16[1,512,4096]{2,1,0:T(8,128)(2,1)} %param.10) | copy-start | bytes 12582916
  56.2 15.6 %copy-start.13 = (bf16[1024]{0:T(1024)(128)(2,1)S(1)}, bf16[1024]{0:T(1024)(128)(2,1)}, u32[]{:S(2)}) copy-start(bf16[1024]{0:T(1024)(128)(2,1)} %param.13) | copy-start | bytes 6148
  57.7 8.6 %copy-start.7 = (f32[4,128,512]{2,1,0:T(8,128)}, f32[4,128,512]{2,1,0:T(8,128)S(1)}, u32[]{:S(2)}) copy-start(f32[4,128,512]{2,1,0:T(8,128)S(1)} %convert_add_fusion.1) | copy-start | bytes 3145732
  58.6 13.2 %collective-permute-start.14 = (bf16[128,512]{1,0:T(8,128)(2,1)}, bf16[128,512]{1,0:T(8,128)(2,1)}, u32[]{:S(2)}, u32[]{:S(2)}) collective-permute-start(bf16[128,512]{1,0:T(8,128)(2,1)} %get-tuple-element.89), channel_id=1, source_target_pairs={{0,6},{1,7},{2,4},{3,5},{4,2},{5,3},{6,0},{7,1},{8,14},{9,15},{10,... | collective-permute-start | bytes 393224 | tf_op jit(solution)/shard_map/ppermute | solution.py:16
  62.1 11.8 %collective-permute-start.13 = (bf16[128,512]{1,0:T(8,128)(2,1)}, bf16[128,512]{1,0:T(8,128)(2,1)}, u32[]{:S(2)}, u32[]{:S(2)}) collective-permute-start(bf16[128,512]{1,0:T(8,128)(2,1)} %get-tuple-element.90), channel_id=1, source_target_pairs={{0,4},{1,5},{2,6},{3,7},{4,0},{5,1},{6,2},{7,3},{8,12},{9,13},{10,... | collective-permute-start | bytes 393224 | tf_op jit(solution)/shard_map/ppermute | solution.py:16
  62.1 11.8 %collective-permute-start.12 = (bf16[128,512]{1,0:T(8,128)(2,1)}, bf16[128,512]{1,0:T(8,128)(2,1)}, u32[]{:S(2)}, u32[]{:S(2)}) collective-permute-start(bf16[128,512]{1,0:T(8,128)(2,1)} %get-tuple-element.91), channel_id=1, source_target_pairs={{0,2},{1,3},{2,0},{3,1},{4,6},{5,7},{6,4},{7,5},{8,10},{9,11},{10,... | collective-permute-start | bytes 393224 | tf_op jit(solution)/shard_map/ppermute | solution.py:16
  68.1 7.8 %collective-permute-start.11 = (bf16[1,256,512]{2,1,0:T(8,128)(2,1)}, bf16[1,256,512]{2,1,0:T(8,128)(2,1)S(1)}, u32[]{:S(2)}, u32[]{:S(2)}) collective-permute-start(bf16[1,256,512]{2,1,0:T(8,128)(2,1)} %add_convert_fusion), channel_id=1, source_target_pairs={{0,8},{8,0},{16,24},{24,16},{1,9},{9,1},{17,25},{25,17},{2,10},{10... | collective-permute-start | bytes 786440 | tf_op jit(solution)/shard_map/ppermute | solution.py:16
  70.9 7.5 %collective-permute-start.10 = (bf16[1,256,512]{2,1,0:T(8,128)(2,1)}, bf16[1,256,512]{2,1,0:T(8,128)(2,1)S(1)}, u32[]{:S(2)}, u32[]{:S(2)}) collective-permute-start(bf16[1,256,512]{2,1,0:T(8,128)(2,1)} %add_convert_fusion.1), channel_id=1, source_target_pairs={{0,16},{8,24},{16,0},{24,8},{1,17},{9,25},{17,1},{25,9},{2,18},{10... | collective-permute-start | bytes 786440 | tf_op jit(solution)/shard_map/ppermute | solution.py:16
  73.8 7.4 %copy-start.14 = (bf16[1024,4]{0,1:T(4,128)(2,1)S(1)}, bf16[1024,4]{0,1:T(4,128)(2,1)}, u32[]{:S(2)}) copy-start(bf16[1024,4]{0,1:T(4,128)(2,1)} %param.14) | copy-start | bytes 24580
  80.6 25.3 %copy-start.10 = (bf16[128,1024]{1,0:T(8,128)(2,1)S(1)}, bf16[128,1024]{1,0:T(8,128)(2,1)}, u32[]{:S(2)}) copy-start(bf16[128,1024]{1,0:T(8,128)(2,1)} %param.12) | copy-start | bytes 786436
  81.2 2.0 collective-permute-start.15
  83.6 7.7 %collective-permute-start.16 = (bf16[128,512]{1,0:T(8,128)(2,1)S(1)}, bf16[128,512]{1,0:T(8,128)(2,1)S(1)}, u32[]{:S(2)}, u32[]{:S(2)}) collective-permute-start(bf16[128,512]{1,0:T(8,128)(2,1)S(1)} %get-tuple-element.86), channel_id=1, source_target_pairs={{0,2},{1,3},{2,0},{3,1},{4,6},{5,7},{6,4},{7,5},{8,10},{9,11},{10,... | collective-permute-start | bytes 393224 | tf_op jit(solution)/shard_map/ppermute | solution.py:16
  85.4 9.6 %collective-permute-start.18 = (bf16[128,512]{1,0:T(8,128)(2,1)S(1)}, bf16[128,512]{1,0:T(8,128)(2,1)S(1)}, u32[]{:S(2)}, u32[]{:S(2)}) collective-permute-start(bf16[128,512]{1,0:T(8,128)(2,1)S(1)} %get-tuple-element.87), channel_id=1, source_target_pairs={{0,6},{1,7},{2,4},{3,5},{4,2},{5,3},{6,0},{7,1},{8,14},{9,15},{10,... | collective-permute-start | bytes 393224 | tf_op jit(solution)/shard_map/ppermute | solution.py:16
  87.7 18.1 %collective-permute-start.17 = (bf16[128,512]{1,0:T(8,128)(2,1)S(1)}, bf16[128,512]{1,0:T(8,128)(2,1)S(1)}, u32[]{:S(2)}, u32[]{:S(2)}) collective-permute-start(bf16[128,512]{1,0:T(8,128)(2,1)S(1)} %get-tuple-element.88), channel_id=1, source_target_pairs={{0,4},{1,5},{2,6},{3,7},{4,0},{5,1},{6,2},{7,3},{8,12},{9,13},{10,... | collective-permute-start | bytes 393224 | tf_op jit(solution)/shard_map/ppermute | solution.py:16
  87.8 18.2 %collective-permute-start.24 = (bf16[128,512]{1,0:T(8,128)(2,1)S(1)}, bf16[128,512]{1,0:T(8,128)(2,1)S(1)}, u32[]{:S(2)}, u32[]{:S(2)}) collective-permute-start(bf16[128,512]{1,0:T(8,128)(2,1)S(1)} %fusion.21.refs_0_), channel_id=1, source_target_pairs={{0,6},{1,7},{2,4},{3,5},{4,2},{5,3},{6,0},{7,1},{8,14},{9,15},{10,... | collective-permute-start | bytes 393224 | tf_op jit(solution)/shard_map/ppermute | solution.py:16
  90.7 20.2 %collective-permute-start.23 = (bf16[128,512]{1,0:T(8,128)(2,1)S(1)}, bf16[128,512]{1,0:T(8,128)(2,1)S(1)}, u32[]{:S(2)}, u32[]{:S(2)}) collective-permute-start(bf16[128,512]{1,0:T(8,128)(2,1)S(1)} %fusion.21.refs_0_), channel_id=1, source_target_pairs={{0,4},{1,5},{2,6},{3,7},{4,0},{5,1},{6,2},{7,3},{8,12},{9,13},{10,... | collective-permute-start | bytes 393224 | tf_op jit(solution)/shard_map/ppermute | solution.py:16
  91.3 19.6 %collective-permute-start.22 = (bf16[128,512]{1,0:T(8,128)(2,1)S(1)}, bf16[128,512]{1,0:T(8,128)(2,1)S(1)}, u32[]{:S(2)}, u32[]{:S(2)}) collective-permute-start(bf16[128,512]{1,0:T(8,128)(2,1)S(1)} %fusion.21.refs_0_), channel_id=1, source_target_pairs={{0,2},{1,3},{2,0},{3,1},{4,6},{5,7},{6,4},{7,5},{8,10},{9,11},{10,... | collective-permute-start | bytes 393224 | tf_op jit(solution)/shard_map/ppermute | solution.py:16
  113.2 23.5 %all-to-all-start.3 = ((bf16[4,400,512]{2,1,0:T(8,128)(2,1)}), bf16[4,400,512]{2,1,0:T(8,128)(2,1)S(1)}, u32[]{:S(2)}, u32[]{:S(2)}) async-start(bf16[4,400,512]{2,1,0:T(8,128)(2,1)} %dispatch.3), calls=%async_computation.3 | async-start | bytes 3276800 | tf_op jit(solution)/shard_map/all_to_all | solution.py:570
  116.8 8.3 %collective-permute-start.21 = (bf16[128,512]{1,0:T(8,128)(2,1)S(1)}, bf16[128,512]{1,0:T(8,128)(2,1)S(1)}, u32[]{:S(2)}, u32[]{:S(2)}) collective-permute-start(bf16[128,512]{1,0:T(8,128)(2,1)S(1)} %fusion.16.refs_0_), channel_id=1, source_target_pairs={{0,6},{1,7},{2,4},{3,5},{4,2},{5,3},{6,0},{7,1},{8,14},{9,15},{10,... | collective-permute-start | bytes 393224 | tf_op jit(solution)/shard_map/ppermute | solution.py:16
  119.5 10.0 %collective-permute-start.20 = (bf16[128,512]{1,0:T(8,128)(2,1)S(1)}, bf16[128,512]{1,0:T(8,128)(2,1)S(1)}, u32[]{:S(2)}, u32[]{:S(2)}) collective-permute-start(bf16[128,512]{1,0:T(8,128)(2,1)S(1)} %fusion.16.refs_0_), channel_id=1, source_target_pairs={{0,4},{1,5},{2,6},{3,7},{4,0},{5,1},{6,2},{7,3},{8,12},{9,13},{10,... | collective-permute-start | bytes 393224 | tf_op jit(solution)/shard_map/ppermute | solution.py:16
  119.5 10.0 %collective-permute-start.19 = (bf16[128,512]{1,0:T(8,128)(2,1)S(1)}, bf16[128,512]{1,0:T(8,128)(2,1)S(1)}, u32[]{:S(2)}, u32[]{:S(2)}) collective-permute-start(bf16[128,512]{1,0:T(8,128)(2,1)S(1)} %fusion.16.refs_0_), channel_id=1, source_target_pairs={{0,2},{1,3},{2,0},{3,1},{4,6},{5,7},{6,4},{7,5},{8,10},{9,11},{10,... | collective-permute-start | bytes 393224 | tf_op jit(solution)/shard_map/ppermute | solution.py:16
  122.0 1.1 copy-start.4
  136.7 3.8 %copy-start.8 = (bf16[4,400,512]{2,1,0:T(8,128)(2,1)}, bf16[4,400,512]{2,1,0:T(8,128)(2,1)S(1)}, u32[]{:S(2)}) copy-start(bf16[4,400,512]{2,1,0:T(8,128)(2,1)S(1)} %all-to-all-done.3.own_ref) | copy-start | bytes 4915204
  136.7 3.8 %collective-permute-start.25 = (bf16[4,400,512]{2,1,0:T(8,128)(2,1)S(1)}, bf16[4,400,512]{2,1,0:T(8,128)(2,1)}, u32[]{:S(2)}, u32[]{:S(2)}) collective-permute-start(bf16[4,400,512]{2,1,0:T(8,128)(2,1)S(1)} %all-to-all-done.3.own_ref), channel_id=1, source_target_pairs={{0,1},{1,0},{2,3},{3,2},{4,5},{5,4},{6,7},{7,6},{8,9},{9,8},{10,11... | collective-permute-start | bytes 4915208 | tf_op jit(solution)/shard_map/ppermute | solution.py:16
  136.7 24.4 %all-to-all-start.2 = ((bf16[4,400,512]{2,1,0:T(8,128)(2,1)}), bf16[4,400,512]{2,1,0:T(8,128)(2,1)S(1)}, u32[]{:S(2)}, u32[]{:S(2)}) async-start(bf16[4,400,512]{2,1,0:T(8,128)(2,1)} %dispatch.2), calls=%async_computation.2 | async-start | bytes 3276800 | tf_op jit(solution)/shard_map/all_to_all | solution.py:570
  161.1 3.5 %copy-start.6 = (bf16[4,400,512]{2,1,0:T(8,128)(2,1)}, bf16[4,400,512]{2,1,0:T(8,128)(2,1)S(1)}, u32[]{:S(2)}) copy-start(bf16[4,400,512]{2,1,0:T(8,128)(2,1)S(1)} %all-to-all-done.2.own_ref) | copy-start | bytes 4915204
  161.1 3.5 %collective-permute-start.26 = (bf16[4,400,512]{2,1,0:T(8,128)(2,1)S(1)}, bf16[4,400,512]{2,1,0:T(8,128)(2,1)S(1)}, u32[]{:S(2)}, u32[]{:S(2)}) collective-permute-start(bf16[4,400,512]{2,1,0:T(8,128)(2,1)S(1)} %all-to-all-done.2.own_ref), channel_id=1, source_target_pairs={{0,1},{1,0},{2,3},{3,2},{4,5},{5,4},{6,7},{7,6},{8,9},{9,8},{10,11... | collective-permute-start | bytes 4915208 | tf_op jit(solution)/shard_map/ppermute | solution.py:16
  164.6 1.2 copy-start.9
where the time goes:
time: 199 us; the launch traced here: 198 us
  waiting for transfers between devices  66.3 us (33%)
  Pallas kernels  58.3 us (29%)
  starting transfers between devices  46.8 us (24%)
  local copies, waits for them, and re-layouts  11 us (6%)
  other arithmetic  11 us (6%)
  matrix products  3.58 us (2%)
    ppermute x27, waiting for transfers between devices, exchange(): return lax.ppermute(value, axis, [(i, i ^ offset) for i in range(size)])  50.4 us
    pallas_call x1, Pallas kernels, per_device(): pl.pallas_call(functools.partial(late_kernel, float(width), tiles), out_s...  32.1 us
    ppermute x27, starting transfers between devices, exchange(): return lax.ppermute(value, axis, [(i, i ^ offset) for i in range(size)])  29.2 us
    pallas_call x1, Pallas kernels, per_device(): pl.pallas_call(functools.partial(early_kernel, tiles), out_shape=(sums, s...  15 us
    all_to_all x2, waiting for transfers between devices, to_experts(): lax.all_to_all(slots[c], 'expert', split_axis=0, concat_axis=0, tiled=True)  10.6 us
    unnamed x35, local copies, waits for them, and re-layouts  10.1 us
    all_to_all x2, starting transfers between devices, to_experts(): lax.all_to_all(slots[c], 'expert', split_axis=0, concat_axis=0, tiled=True)  7.32 us
    convert_element_type x4, other arithmetic, branch_sends(): stacked.append(held[c, h](chosen).astype(jnp.bfloat16))  5.92 us
  transfers between devices with their start and end apart: 31, of which 20 were waited for; matrix products, arithmetic and copies ran while one was open for 6% of the time, Pallas kernels for 11%

commit v1 on v0

--- a/solution.py
+++ b/solution.py
@@ -91,7 +91,7 @@
         in_specs=[smem(), source_spec],
         out_specs=(spec, spec),
         scratch_shapes=[pltpu.SemaphoreType.DMA((2 * others,))],
-        compiler_params=params(),
+        compiler_params=params(61),
         name="pack",
     )(position, branch)
 
@@ -469,6 +469,22 @@
     keep(1, after(position, packed1))
     pieces = [exchange(own_share, "expert", k) if k else own_share for k in range(experts)]
     pieces, packed1 = lax.optimization_barrier((pieces, packed1))
+    signs = pl.pallas_call(
+        functools.partial(signs_kernel, experts),
+        out_shape=jax.ShapeDtypeStruct((blocks, capacity, lanes), jnp.float32),
+        in_specs=[smem(), whole(ids_all.shape)],
+        out_specs=whole((blocks, capacity, lanes)),
+        grid=(1,),
+        compiler_params=params(),
+        name="signs",
+    )(position, ids_all).reshape(planes, 2, capacity, lanes)
+
+    gate_view = gate_w.reshape(experts, CHUNKS, part, units)
+    up_view = up_w.reshape(experts, CHUNKS, part, units)
+    tile = min(256, units)
+    stretch = min(512, units)
+    tiles = units // tile
+    pieces, signs = lax.optimization_barrier((pieces, signs))
     side_shape = (planes, experts, quarter, features)
     sides = pl.pallas_call(
         sides_kernel,
@@ -480,21 +496,6 @@
         name="sides",
     )(position, *[piece.reshape(planes, 2, quarter, features) for piece in pieces])
     sides = [side.reshape(planes * tokens, features) for side in sides]
-    signs = pl.pallas_call(
-        functools.partial(signs_kernel, experts),
-        out_shape=jax.ShapeDtypeStruct((blocks, capacity, lanes), jnp.float32),
-        in_specs=[smem(), whole(ids_all.shape)],
-        out_specs=whole((blocks, capacity, lanes)),
-        grid=(1,),
-        compiler_params=params(),
-        name="signs",
-    )(position, ids_all).reshape(planes, 2, capacity, lanes)
-
-    gate_view = gate_w.reshape(experts, CHUNKS, part, units)
-    up_view = up_w.reshape(experts, CHUNKS, part, units)
-    tile = min(256, units)
-    stretch = min(512, units)
-    tiles = units // tile
     def pair_of(merged):
         def attend(rows):
             out = jnp.dot(rows, merged, preferred_element_type=jnp.float32)
@@ -557,10 +558,10 @@
         name="join",
     )(merged0, merged1)
     pair1 = pair_of(merged1)
-    sends1 = plane_sends(pair1)
+    sends1 = after(plane_sends(pair1), tokens0)
     arrived1 = plane_exchange(sends1)
 
-    scaled1 = scaled_of(1, pair1, arrived1)
+    scaled1 = scaled_of(1, pair1, after(arrived1, merged_out))
     slots0 = slots_of(0, after(tokens0, scaled1))
     tokens1 = [scaled1] + plane_exchange([scaled1] * (planes - 1))
     slots1 = slots_of(1, tokens1)

time: 199 us -> 315 us (1.58)
  Pallas kernels: 58.3 us -> 189 us
  waiting for transfers between devices: 66.3 us -> 55.4 us
  local copies, waits for them, and re-layouts: 11 us -> 4.79 us
    pallas_call x4, Pallas kernels: 3.41 us -> 134 us  [pack(): pl.pallas_call(functools.partial(pack_kernel, c, flip), out_shape=(jax.Sh...]
    ppermute x27, waiting for transfers between devices: 50.4 us -> 43.7 us  [exchange(): return lax.ppermute(value, axis, [(i, i ^ offset) for i in range(size)])]
    unnamed x35, local copies, waits for them, and re-layouts: 10.1 us -> 3.9 us
    all_to_all x2, waiting for transfers between devices: 10.6 us -> 7.04 us  [to_experts(): lax.all_to_all(slots[c], 'expert', split_axis=0, concat_axis=0, tiled=True)]
  transfers between devices with their start and end apart: 31 -> 31, of which waited for: 20 -> 13; matrix products, arithmetic and copies ran while one was open for 6% -> 4% of each run, Pallas kernels for 11% -> 38%
where the time goes in v1:
time: 315 us; the launch traced here: 314 us
  Pallas kernels  189 us (60%)
  waiting for transfers between devices  55.4 us (18%)
  starting transfers between devices  47.9 us (15%)
  other arithmetic  12.6 us (4%)
  local copies, waits for them, and re-layouts  4.79 us (2%)
    pallas_call x4, Pallas kernels, pack(): pl.pallas_call(functools.partial(pack_kernel, c, flip), out_shape=(jax.Sh...  134 us
    ppermute x27, waiting for transfers between devices, exchange(): return lax.ppermute(value, axis, [(i, i ^ offset) for i in range(size)])  43.7 us
    pallas_call x1, Pallas kernels, per_device(): pl.pallas_call(functools.partial(late_kernel, float(width), tiles), out_s...  32.1 us
    ppermute x27, starting transfers between devices, exchange(): return lax.ppermute(value, axis, [(i, i ^ offset) for i in range(size)])  29.6 us
    pallas_call x1, Pallas kernels, per_device(): pl.pallas_call(functools.partial(early_kernel, tiles), out_shape=(sums, s...  15 us
    all_to_all x2, starting transfers between devices, to_experts(): lax.all_to_all(slots[c], 'expert', split_axis=0, concat_axis=0, tiled=True)  8.14 us
    all_to_all x2, waiting for transfers between devices, to_experts(): lax.all_to_all(slots[c], 'expert', split_axis=0, concat_axis=0, tiled=True)  7.04 us
    convert_element_type x4, other arithmetic, branch_sends(): stacked.append(held[c, h](chosen).astype(jnp.bfloat16))  6.87 us
  transfers between devices with their start and end apart: 31, of which 13 were waited for; matrix products, arithmetic and copies ran while one was open for 4% of the time, Pallas kernels for 38%

profile of v1, /device:TPU:0, one launch (start us, length us, event | category | flops | bytes accessed | tf_op | source)
XLA Modules:
  0.0 313.9 jit_solution(11421339561235775209)
XLA Ops:
  0.7 5.3 %all-to-all-start = ((bf16[4,32,1024]{2,1,0:T(8,128)(2,1)}), bf16[4,32,1024]{2,1,0:T(8,128)(2,1)S(1)}, u32[]{:S(2)}, u32[]{:S(2)}) async-start(bf16[4,32,1024]{2,1,0:T(8,128)(2,1)} %bitcast.110), calls=%async_computation | async-start | bytes 524288 | tf_op jit(solution)/shard_map/all_to_all | solution.py:441
  6.0 0.7 pad_add_fusion.position_ref
  6.6 4.7 %all-to-all-done.shares_ref = bf16[4,32,1024]{2,1,0:T(8,128)(2,1)S(1)} async-done(((bf16[4,32,1024]{2,1,0:T(8,128)(2,1)}), bf16[4,32,1024]{2,1,0:T(8,128)(2,1)S(1)}, u32[]{:S(2)}, u32[]{:S(2)}) %all-to-all-start) | async-done | bytes 262176 | tf_op jit(solution)/shard_map/all_to_all | solution.py:441
  11.3 33.6 %pack.5 = (bf16[2,256,512]{2,1,0:T(8,128)(2,1)}, bf16[2,256,512]{2,1,0:T(8,128)(2,1)}) custom-call(s32[3]{0:T(128)} %pad_add_fusion.position_ref, bf16[512,4096]{1,0:T(8,128)(2,1)} %bitcast.101), custom_call_target="tpu_custom_call" | custom-call | tf_op jit(solution)/shard_map/pack/pallas_call | solution.py:88
  44.9 1.3 collective-permute-start
  46.2 0.6 collective-permute-start.1
  46.9 0.8 spread.1
  47.7 4.9 %all-to-all-start.1 = ((bf16[8,48,512]{2,1,0:T(8,128)(2,1)}), bf16[8,48,512]{2,1,0:T(8,128)(2,1)S(1)}, u32[]{:S(2)}, u32[]{:S(2)}) async-start(bf16[8,48,512]{2,1,0:T(8,128)(2,1)} %spread.1), calls=%async_computation.1 | async-start | bytes 786432 | tf_op jit(solution)/shard_map/all_to_all | solution.py:458
  52.5 33.6 %pack.4 = (bf16[2,256,512]{2,1,0:T(8,128)(2,1)}, bf16[2,256,512]{2,1,0:T(8,128)(2,1)}) custom-call(s32[3]{0:T(128)} %pad_add_fusion.position_ref, bf16[512,4096]{1,0:T(8,128)(2,1)} %bitcast.102), custom_call_target="tpu_custom_call" | custom-call | tf_op jit(solution)/shard_map/pack/pallas_call | solution.py:88
  86.1 1.7 add_convert_fusion.2
  87.9 1.5 collective-permute-start.3
  89.3 1.7 add_convert_fusion.3
  91.0 0.8 collective-permute-start.2
  91.8 33.6 %pack.6 = (bf16[2,256,512]{2,1,0:T(8,128)(2,1)}, bf16[2,256,512]{2,1,0:T(8,128)(2,1)}) custom-call(s32[3]{0:T(128)} %pad_add_fusion.position_ref, bf16[512,4096]{1,0:T(8,128)(2,1)} %bitcast.103), custom_call_target="tpu_custom_call" | custom-call | tf_op jit(solution)/shard_map/pack/pallas_call | solution.py:88
  125.5 1.3 collective-permute-start.6
  126.8 1.5 collective-permute-start.5
  128.3 0.8 collective-permute-start.4
  129.0 0.8 signs.1
  129.9 1.3 add_bitcast_fusion.2
  131.3 4.4 %collective-permute-done.6 = bf16[8,32,512]{2,1,0:T(8,128)(2,1)S(1)} collective-permute-done((bf16[8,32,512]{2,1,0:T(8,128)(2,1)S(1)}, bf16[8,32,512]{2,1,0:T(8,128)(2,1)S(1)}, u32[]{:S(2)}, u32[]{:S(2)}) %collective-permute-start.6) | collective-permute-done | bytes 262176 | tf_op jit(solution)/shard_map/ppermute | solution.py:16
  135.7 4.6 %collective-permute-done.5 = bf16[8,32,512]{2,1,0:T(8,128)(2,1)S(1)} collective-permute-done((bf16[8,32,512]{2,1,0:T(8,128)(2,1)S(1)}, bf16[8,32,512]{2,1,0:T(8,128)(2,1)S(1)}, u32[]{:S(2)}, u32[]{:S(2)}) %collective-permute-start.5) | collective-permute-done | bytes 262176 | tf_op jit(solution)/shard_map/ppermute | solution.py:16
  140.2 0.6 sides.1
  141.4 1.3 collective-permute-start.7
  142.7 0.6 collective-permute-start.8
  143.3 33.6 %pack.7 = (bf16[2,256,512]{2,1,0:T(8,128)(2,1)}, bf16[2,256,512]{2,1,0:T(8,128)(2,1)}) custom-call(s32[3]{0:T(128)} %pad_add_fusion.position_ref, bf16[512,4096]{1,0:T(8,128)(2,1)} %bitcast.104), custom_call_target="tpu_custom_call" | custom-call | tf_op jit(solution)/shard_map/pack/pallas_call | solution.py:88
  177.0 0.8 copy-done.5
  177.7 1.5 convert_add_fusion.1
  179.2 0.8 fusion.24
  180.0 3.5 %collective-permute-start.14 = (bf16[128,512]{1,0:T(8,128)(2,1)}, bf16[128,512]{1,0:T(8,128)(2,1)S(1)}, u32[]{:S(2)}, u32[]{:S(2)}) collective-permute-start(bf16[128,512]{1,0:T(8,128)(2,1)} %get-tuple-element.111), channel_id=1, source_target_pairs={{0,6},{1,7},{2,4},{3,5},{4,2},{5,3},{6,0},{7,1},{8,14},{9,15},{10,... | collective-permute-start | bytes 393224 | tf_op jit(solution)/shard_map/ppermute | solution.py:16
  183.5 0.9 collective-permute-start.12
  184.4 1.7 add_convert_fusion
  186.1 1.4 collective-permute-start.11
  187.6 1.7 add_convert_fusion.1
  189.3 0.8 collective-permute-start.10
  190.1 5.0 %collective-permute-done.13 = bf16[128,512]{1,0:T(8,128)(2,1)S(1)} collective-permute-done((bf16[128,512]{1,0:T(8,128)(2,1)}, bf16[128,512]{1,0:T(8,128)(2,1)S(1)}, u32[]{:S(2)}, u32[]{:S(2)}) %collective-permute-start.13) | collective-permute-done | bytes 131104 | tf_op jit(solution)/shard_map/ppermute | solution.py:16
  195.1 0.6 copy-done.11
  195.7 1.1 fusion.21.refs_0_
  196.8 1.1 add_bitcast_fusion
  197.9 1.2 add_bitcast_fusion.1
  199.8 3.3 %collective-permute-start.18 = (bf16[128,512]{1,0:T(8,128)(2,1)S(1)}, bf16[128,512]{1,0:T(8,128)(2,1)S(1)}, u32[]{:S(2)}, u32[]{:S(2)}) collective-permute-start(bf16[128,512]{1,0:T(8,128)(2,1)S(1)} %fusion.21.refs_0_), channel_id=1, source_target_pairs={{0,6},{1,7},{2,4},{3,5},{4,2},{5,3},{6,0},{7,1},{8,14},{9,15},{10,... | collective-permute-start | bytes 393224 | tf_op jit(solution)/shard_map/ppermute | solution.py:16
  203.1 1.1 collective-permute-start.16
  204.8 3.3 %collective-permute-done.18.refs_3_ = bf16[128,512]{1,0:T(8,128)(2,1)S(1)} collective-permute-done((bf16[128,512]{1,0:T(8,128)(2,1)S(1)}, bf16[128,512]{1,0:T(8,128)(2,1)S(1)}, u32[]{:S(2)}, u32[]{:S(2)}) %collective-permute-start.18) | collective-permute-done | bytes 131104 | tf_op jit(solution)/shard_map/ppermute | solution.py:16
  208.1 6.7 %collective-permute-done.17.refs_2_ = bf16[128,512]{1,0:T(8,128)(2,1)S(1)} collective-permute-done((bf16[128,512]{1,0:T(8,128)(2,1)S(1)}, bf16[128,512]{1,0:T(8,128)(2,1)S(1)}, u32[]{:S(2)}, u32[]{:S(2)}) %collective-permute-start.17) | collective-permute-done | bytes 131104 | tf_op jit(solution)/shard_map/ppermute | solution.py:16
  214.8 2.9 collective-permute-start.20
  217.7 1.5 collective-permute-start.21
  219.2 1.1 join.1
  220.2 1.6 collective-permute-done.19
  221.9 5.8 %collective-permute-done.20 = bf16[128,512]{1,0:T(8,128)(2,1)S(1)} collective-permute-done((bf16[128,512]{1,0:T(8,128)(2,1)S(1)}, bf16[128,512]{1,0:T(8,128)(2,1)S(1)}, u32[]{:S(2)}, u32[]{:S(2)}) %collective-permute-start.20) | collective-permute-done | bytes 131104 | tf_op jit(solution)/shard_map/ppermute | solution.py:16
  227.8 2.3 dispatch.3
  230.1 4.4 %all-to-all-start.3 = ((bf16[4,400,512]{2,1,0:T(8,128)(2,1)}), bf16[4,400,512]{2,1,0:T(8,128)(2,1)}, u32[]{:S(2)}, u32[]{:S(2)}) async-start(bf16[4,400,512]{2,1,0:T(8,128)(2,1)} %dispatch.3), calls=%async_computation.3 | async-start | bytes 3276800 | tf_op jit(solution)/shard_map/all_to_all | solution.py:571
  234.5 2.4 collective-permute-start.24
  236.9 1.2 collective-permute-start.23
  238.1 0.9 collective-permute-start.22
  238.9 3.8 %collective-permute-done.24.refs_3_ = bf16[128,512]{1,0:T(8,128)(2,1)S(1)} collective-permute-done((bf16[128,512]{1,0:T(8,128)(2,1)S(1)}, bf16[128,512]{1,0:T(8,128)(2,1)S(1)}, u32[]{:S(2)}, u32[]{:S(2)}) %collective-permute-start.24) | collective-permute-done | bytes 131104 | tf_op jit(solution)/shard_map/ppermute | solution.py:16
  242.8 4.9 %collective-permute-done.23.refs_2_ = bf16[128,512]{1,0:T(8,128)(2,1)S(1)} collective-permute-done((bf16[128,512]{1,0:T(8,128)(2,1)S(1)}, bf16[128,512]{1,0:T(8,128)(2,1)S(1)}, u32[]{:S(2)}, u32[]{:S(2)}) %collective-permute-start.23) | collective-permute-done | bytes 131104 | tf_op jit(solution)/shard_map/ppermute | solution.py:16
  247.7 2.3 dispatch.2
  250.0 2.5 all-to-all-done.3.own_ref
  252.4 3.8 %all-to-all-start.2 = ((bf16[4,400,512]{2,1,0:T(8,128)(2,1)}), bf16[4,400,512]{2,1,0:T(8,128)(2,1)S(1)}, u32[]{:S(2)}, u32[]{:S(2)}) async-start(bf16[4,400,512]{2,1,0:T(8,128)(2,1)} %dispatch.2), calls=%async_computation.2 | async-start | bytes 3276800 | tf_op jit(solution)/shard_map/all_to_all | solution.py:571
  256.2 1.2 copy-done.14
  257.4 15.0 %early.1 = (f32[768,1024]{1,0:T(8,128)}, f32[768,1024]{1,0:T(8,128)}, f32[768,16]{1,0:T(8,128)}, bf16[4,512,768]{2,1,0:T(8,128)(2,1)}) custom-call(bf16[4,400,512]{2,1,0:T(8,128)(2,1)} %all-to-all-done.3.own_ref, bf16[4,400,512]{2,1,0:T(8,128)(2,1)} %copy-done.14, bf16[4,2,512,1024]{3,2,1,0:T(8,128)(2,1)} %bitcast.105, bf16[4,2,512,1024]{3,2,1,0:T(8,128)(2,1)} %bitcast.107), custom_call_target="tpu_custom_call" | custom-call | flops 6442450944 | bytes 8388608 | tf_op jit(solution)/shard_map/early/pallas_call | solution.py:583
  272.3 4.5 %all-to-all-done.2.own_ref = bf16[4,400,512]{2,1,0:T(8,128)(2,1)S(1)} async-done(((bf16[4,400,512]{2,1,0:T(8,128)(2,1)}), bf16[4,400,512]{2,1,0:T(8,128)(2,1)S(1)}, u32[]{:S(2)}, u32[]{:S(2)}) %all-to-all-start.2) | async-done | bytes 1638432 | tf_op jit(solution)/shard_map/all_to_all | solution.py:571
  276.9 3.5 %collective-permute-done.26.other_ref = bf16[4,400,512]{2,1,0:T(8,128)(2,1)S(1)} collective-permute-done((bf16[4,400,512]{2,1,0:T(8,128)(2,1)S(1)}, bf16[4,400,512]{2,1,0:T(8,128)(2,1)S(1)}, u32[]{:S(2)}, u32[]{:S(2)}) %collective-permute-start.26) | collective-permute-done | bytes 1638432 | tf_op jit(solution)/shard_map/ppermute | solution.py:16
  280.4 1.2 copy-done.4
  281.6 32.1 %late.1 = (bf16[4,2,96,1024]{3,2,1,0:T(8,128)(2,1)}, bf16[4,1024,1024]{2,1,0:T(8,128)(2,1)}, bf16[4,1024,1024]{2,1,0:T(8,128)(2,1)}) custom-call(s32[3]{0:T(128)} %pad_add_fusion.position_ref, bf16[4,400,512]{2,1,0:T(8,128)(2,1)} %copy-done.3, bf16[4,400,512]{2,1,0:T(8,128)(2,1)} %copy-done.4, bf16[4,512,768]{2,1,0:T(8,128)(2,1)} %get-tuple-element.103.turned_ref, ...), custom_call_target="tpu_custom_call" | custom-call | tf_op jit(solution)/shard_map/late/pallas_call | solution.py:622
  (72 shorter events, 2.1 us)
Async XLA Ops:
  0.6 46.2 %copy-start.15 = (s32[128,2]{0,1:T(2,128)S(1)}, s32[128,2]{0,1:T(2,128)}, u32[]{:S(2)}) copy-start(s32[128,2]{0,1:T(2,128)} %param.17) | copy-start | bytes 3076
  0.6 46.2 %copy-start.16 = (s32[128,2]{0,1:T(2,128)S(1)}, s32[128,2]{0,1:T(2,128)}, u32[]{:S(2)}) copy-start(s32[128,2]{0,1:T(2,128)} %param.18) | copy-start | bytes 3076
  0.7 10.7 %all-to-all-start = ((bf16[4,32,1024]{2,1,0:T(8,128)(2,1)}), bf16[4,32,1024]{2,1,0:T(8,128)(2,1)S(1)}, u32[]{:S(2)}, u32[]{:S(2)}) async-start(bf16[4,32,1024]{2,1,0:T(8,128)(2,1)} %bitcast.110), calls=%async_computation | async-start | bytes 524288 | tf_op jit(solution)/shard_map/all_to_all | solution.py:441
  44.9 41.2 %collective-permute-start = (bf16[2,256,512]{2,1,0:T(8,128)(2,1)}, bf16[2,256,512]{2,1,0:T(8,128)(2,1)S(1)}, u32[]{:S(2)}, u32[]{:S(2)}) collective-permute-start(bf16[2,256,512]{2,1,0:T(8,128)(2,1)} %get-tuple-element.59), channel_id=1, source_target_pairs={{0,8},{8,0},{16,24},{24,16},{1,9},{9,1},{17,25},{25,17},{2,10},{10... | collective-permute-start | bytes 1572872 | tf_op jit(solution)/shard_map/ppermute | solution.py:16
  46.2 39.9 %collective-permute-start.1 = (bf16[2,256,512]{2,1,0:T(8,128)(2,1)}, bf16[2,256,512]{2,1,0:T(8,128)(2,1)S(1)}, u32[]{:S(2)}, u32[]{:S(2)}) collective-permute-start(bf16[2,256,512]{2,1,0:T(8,128)(2,1)} %get-tuple-element.60), channel_id=1, source_target_pairs={{0,16},{8,24},{16,0},{24,8},{1,17},{9,25},{17,1},{25,9},{2,18},{10... | collective-permute-start | bytes 1572872 | tf_op jit(solution)/shard_map/ppermute | solution.py:16
  47.7 77.7 %all-to-all-start.1 = ((bf16[8,48,512]{2,1,0:T(8,128)(2,1)}), bf16[8,48,512]{2,1,0:T(8,128)(2,1)S(1)}, u32[]{:S(2)}, u32[]{:S(2)}) async-start(bf16[8,48,512]{2,1,0:T(8,128)(2,1)} %spread.1), calls=%async_computation.1 | async-start | bytes 786432 | tf_op jit(solution)/shard_map/all_to_all | solution.py:458
  86.1 42.9 %copy-start.1 = (s32[3]{0:T(128)S(1)}, s32[3]{0:T(128)}, u32[]{:S(2)}) copy-start(s32[3]{0:T(128)} %pad_add_fusion.position_ref) | copy-start | bytes 40
  87.9 42.0 %copy-start.8 = (bf16[2,256,512]{2,1,0:T(8,128)(2,1)S(1)}, bf16[2,256,512]{2,1,0:T(8,128)(2,1)}, u32[]{:S(2)}) copy-start(bf16[2,256,512]{2,1,0:T(8,128)(2,1)} %get-tuple-element.57) | copy-start | bytes 1572868
  87.9 42.0 %copy-start.9 = (bf16[2,256,512]{2,1,0:T(8,128)(2,1)S(1)}, bf16[2,256,512]{2,1,0:T(8,128)(2,1)}, u32[]{:S(2)}) copy-start(bf16[2,256,512]{2,1,0:T(8,128)(2,1)} %get-tuple-element.62) | copy-start | bytes 1572868
  87.9 37.5 %collective-permute-start.3 = (bf16[1,256,512]{2,1,0:T(8,128)(2,1)}, bf16[1,256,512]{2,1,0:T(8,128)(2,1)S(1)}, u32[]{:S(2)}, u32[]{:S(2)}) collective-permute-start(bf16[1,256,512]{2,1,0:T(8,128)(2,1)} %add_convert_fusion.2), channel_id=1, source_target_pairs={{0,8},{8,0},{16,24},{24,16},{1,9},{9,1},{17,25},{25,17},{2,10},{10... | collective-permute-start | bytes 786440 | tf_op jit(solution)/shard_map/ppermute | solution.py:16
  91.0 34.4 %collective-permute-start.2 = (bf16[1,256,512]{2,1,0:T(8,128)(2,1)}, bf16[1,256,512]{2,1,0:T(8,128)(2,1)}, u32[]{:S(2)}, u32[]{:S(2)}) collective-permute-start(bf16[1,256,512]{2,1,0:T(8,128)(2,1)} %add_convert_fusion.3), channel_id=1, source_target_pairs={{0,16},{8,24},{16,0},{24,8},{1,17},{9,25},{17,1},{25,9},{2,18},{10... | collective-permute-start | bytes 786440 | tf_op jit(solution)/shard_map/ppermute | solution.py:16
  125.5 10.2 %collective-permute-start.6 = (bf16[8,32,512]{2,1,0:T(8,128)(2,1)S(1)}, bf16[8,32,512]{2,1,0:T(8,128)(2,1)S(1)}, u32[]{:S(2)}, u32[]{:S(2)}) collective-permute-start(bf16[8,32,512]{2,1,0:T(8,128)(2,1)S(1)} %slice.18), channel_id=1, source_target_pairs={{0,24},{8,16},{16,8},{24,0},{1,25},{9,17},{17,9},{25,1},{2,26},{10... | collective-permute-start | bytes 786440 | tf_op jit(solution)/shard_map/ppermute | solution.py:16
  126.8 13.4 %collective-permute-start.5 = (bf16[8,32,512]{2,1,0:T(8,128)(2,1)S(1)}, bf16[8,32,512]{2,1,0:T(8,128)(2,1)S(1)}, u32[]{:S(2)}, u32[]{:S(2)}) collective-permute-start(bf16[8,32,512]{2,1,0:T(8,128)(2,1)S(1)} %slice.18), channel_id=1, source_target_pairs={{0,16},{8,24},{16,0},{24,8},{1,17},{9,25},{17,1},{25,9},{2,18},{10... | collective-permute-start | bytes 786440 | tf_op jit(solution)/shard_map/ppermute | solution.py:16
  128.3 11.9 %collective-permute-start.4 = (bf16[8,32,512]{2,1,0:T(8,128)(2,1)S(1)}, bf16[8,32,512]{2,1,0:T(8,128)(2,1)S(1)}, u32[]{:S(2)}, u32[]{:S(2)}) collective-permute-start(bf16[8,32,512]{2,1,0:T(8,128)(2,1)S(1)} %slice.18), channel_id=1, source_target_pairs={{0,8},{8,0},{16,24},{24,16},{1,9},{9,1},{17,25},{25,17},{2,10},{10... | collective-permute-start | bytes 786440 | tf_op jit(solution)/shard_map/ppermute | solution.py:16
  129.9 10.4 %copy-start = (f32[8,96,16]{2,1,0:T(8,128)}, f32[8,96,16]{2,1,0:T(8,128)S(1)}, u32[]{:S(2)}) copy-start(f32[8,96,16]{2,1,0:T(8,128)S(1)} %signs.1) | copy-start | bytes 147460
  141.3 35.7 %collective-permute-start.9 = (bf16[4,128,512]{2,1,0:T(8,128)(2,1)S(1)}, bf16[4,128,512]{2,1,0:T(8,128)(2,1)S(1)}, u32[]{:S(2)}, u32[]{:S(2)}) collective-permute-start(bf16[4,128,512]{2,1,0:T(8,128)(2,1)S(1)} %convolution_convert_fusion.1), channel_id=1, source_target_pairs={{0,1},{1,0},{2,3},{3,2},{4,5},{5,4},{6,7},{7,6},{8,9},{9,8},{10,11... | collective-permute-start | bytes 1572872 | tf_op jit(solution)/shard_map/ppermute | solution.py:16
  141.4 43.1 %collective-permute-start.7 = (bf16[2,256,512]{2,1,0:T(8,128)(2,1)}, bf16[2,256,512]{2,1,0:T(8,128)(2,1)}, u32[]{:S(2)}, u32[]{:S(2)}) collective-permute-start(bf16[2,256,512]{2,1,0:T(8,128)(2,1)} %get-tuple-element.71), channel_id=1, source_target_pairs={{0,8},{8,0},{16,24},{24,16},{1,9},{9,1},{17,25},{25,17},{2,10},{10... | collective-permute-start | bytes 1572872 | tf_op jit(solution)/shard_map/ppermute | solution.py:16
  142.7 41.7 %collective-permute-start.8 = (bf16[2,256,512]{2,1,0:T(8,128)(2,1)}, bf16[2,256,512]{2,1,0:T(8,128)(2,1)}, u32[]{:S(2)}, u32[]{:S(2)}) collective-permute-start(bf16[2,256,512]{2,1,0:T(8,128)(2,1)} %get-tuple-element.72), channel_id=1, source_target_pairs={{0,16},{8,24},{16,0},{24,8},{1,17},{9,25},{17,1},{25,9},{2,18},{10... | collective-permute-start | bytes 1572872 | tf_op jit(solution)/shard_map/ppermute | solution.py:16
  176.9 13.2 %copy-start.12 = (bf16[1024]{0:T(1024)(128)(2,1)S(1)}, bf16[1024]{0:T(1024)(128)(2,1)}, u32[]{:S(2)}) copy-start(bf16[1024]{0:T(1024)(128)(2,1)} %param.13) | copy-start | bytes 6148
  176.9 18.8 %copy-start.10 = (bf16[128,1024]{1,0:T(8,128)(2,1)S(1)}, bf16[128,1024]{1,0:T(8,128)(2,1)}, u32[]{:S(2)}) copy-start(bf16[128,1024]{1,0:T(8,128)(2,1)} %param.12) | copy-start | bytes 786436
  176.9 7.5 %copy-start.7 = (bf16[2,256,512]{2,1,0:T(8,128)(2,1)S(1)}, bf16[2,256,512]{2,1,0:T(8,128)(2,1)}, u32[]{:S(2)}) copy-start(bf16[2,256,512]{2,1,0:T(8,128)(2,1)} %get-tuple-element.84) | copy-start | bytes 1572868
  176.9 10.6 %copy-start.6 = (bf16[2,256,512]{2,1,0:T(8,128)(2,1)S(1)}, bf16[2,256,512]{2,1,0:T(8,128)(2,1)}, u32[]{:S(2)}) copy-start(bf16[2,256,512]{2,1,0:T(8,128)(2,1)} %get-tuple-element.69) | copy-start | bytes 1572868
  176.9 0.8 copy-start.5
  180.0 10.0 %collective-permute-start.14 = (bf16[128,512]{1,0:T(8,128)(2,1)}, bf16[128,512]{1,0:T(8,128)(2,1)S(1)}, u32[]{:S(2)}, u32[]{:S(2)}) collective-permute-start(bf16[128,512]{1,0:T(8,128)(2,1)} %get-tuple-element.111), channel_id=1, source_target_pairs={{0,6},{1,7},{2,4},{3,5},{4,2},{5,3},{6,0},{7,1},{8,14},{9,15},{10,... | collective-permute-start | bytes 393224 | tf_op jit(solution)/shard_map/ppermute | solution.py:16
  183.5 11.6 %collective-permute-start.13 = (bf16[128,512]{1,0:T(8,128)(2,1)}, bf16[128,512]{1,0:T(8,128)(2,1)S(1)}, u32[]{:S(2)}, u32[]{:S(2)}) collective-permute-start(bf16[128,512]{1,0:T(8,128)(2,1)} %get-tuple-element.112), channel_id=1, source_target_pairs={{0,4},{1,5},{2,6},{3,7},{4,0},{5,1},{6,2},{7,3},{8,12},{9,13},{10,... | collective-permute-start | bytes 393224 | tf_op jit(solution)/shard_map/ppermute | solution.py:16
  183.5 11.6 %collective-permute-start.12 = (bf16[128,512]{1,0:T(8,128)(2,1)}, bf16[128,512]{1,0:T(8,128)(2,1)}, u32[]{:S(2)}, u32[]{:S(2)}) collective-permute-start(bf16[128,512]{1,0:T(8,128)(2,1)} %get-tuple-element.113), channel_id=1, source_target_pairs={{0,2},{1,3},{2,0},{3,1},{4,6},{5,7},{6,4},{7,5},{8,10},{9,11},{10,... | collective-permute-start | bytes 393224 | tf_op jit(solution)/shard_map/ppermute | solution.py:16
  186.1 10.6 %collective-permute-start.11 = (bf16[1,256,512]{2,1,0:T(8,128)(2,1)}, bf16[1,256,512]{2,1,0:T(8,128)(2,1)S(1)}, u32[]{:S(2)}, u32[]{:S(2)}) collective-permute-start(bf16[1,256,512]{2,1,0:T(8,128)(2,1)} %add_convert_fusion), channel_id=1, source_target_pairs={{0,8},{8,0},{16,24},{24,16},{1,9},{9,1},{17,25},{25,17},{2,10},{10... | collective-permute-start | bytes 786440 | tf_op jit(solution)/shard_map/ppermute | solution.py:16
  189.3 7.5 %collective-permute-start.10 = (bf16[1,256,512]{2,1,0:T(8,128)(2,1)}, bf16[1,256,512]{2,1,0:T(8,128)(2,1)}, u32[]{:S(2)}, u32[]{:S(2)}) collective-permute-start(bf16[1,256,512]{2,1,0:T(8,128)(2,1)} %add_convert_fusion.1), channel_id=1, source_target_pairs={{0,16},{8,24},{16,0},{24,8},{1,17},{9,25},{17,1},{25,9},{2,18},{10... | collective-permute-start | bytes 786440 | tf_op jit(solution)/shard_map/ppermute | solution.py:16
  195.0 0.6 copy-start.11
  199.1 20.0 %copy-start.13 = (bf16[1024,4]{0,1:T(4,128)(2,1)S(1)}, bf16[1024,4]{0,1:T(4,128)(2,1)}, u32[]{:S(2)}) copy-start(bf16[1024,4]{0,1:T(4,128)(2,1)} %param.14) | copy-start | bytes 24580
  199.7 28.1 %copy-start.2 = (s32[3]{0:T(128)S(1)}, s32[3]{0:T(128)}, u32[]{:S(2)}) copy-start(s32[3]{0:T(128)} %pad_add_fusion.position_ref) | copy-start | bytes 40
  199.7 4.5 %collective-permute-start.15 = (bf16[4,128,512]{2,1,0:T(8,128)(2,1)S(1)}, bf16[4,128,512]{2,1,0:T(8,128)(2,1)S(1)}, u32[]{:S(2)}, u32[]{:S(2)}) collective-permute-start(bf16[4,128,512]{2,1,0:T(8,128)(2,1)S(1)} %convolution_convert_fusion), channel_id=1, source_target_pairs={{0,1},{1,0},{2,3},{3,2},{4,5},{5,4},{6,7},{7,6},{8,9},{9,8},{10,11... | collective-permute-start | bytes 1572872 | tf_op jit(solution)/shard_map/ppermute | solution.py:16
  199.8 8.3 %collective-permute-start.18 = (bf16[128,512]{1,0:T(8,128)(2,1)S(1)}, bf16[128,512]{1,0:T(8,128)(2,1)S(1)}, u32[]{:S(2)}, u32[]{:S(2)}) collective-permute-start(bf16[128,512]{1,0:T(8,128)(2,1)S(1)} %fusion.21.refs_0_), channel_id=1, source_target_pairs={{0,6},{1,7},{2,4},{3,5},{4,2},{5,3},{6,0},{7,1},{8,14},{9,15},{10,... | collective-permute-start | bytes 393224 | tf_op jit(solution)/shard_map/ppermute | solution.py:16
  203.1 11.6 %collective-permute-start.17 = (bf16[128,512]{1,0:T(8,128)(2,1)S(1)}, bf16[128,512]{1,0:T(8,128)(2,1)S(1)}, u32[]{:S(2)}, u32[]{:S(2)}) collective-permute-start(bf16[128,512]{1,0:T(8,128)(2,1)S(1)} %fusion.21.refs_0_), channel_id=1, source_target_pairs={{0,4},{1,5},{2,6},{3,7},{4,0},{5,1},{6,2},{7,3},{8,12},{9,13},{10,... | collective-permute-start | bytes 393224 | tf_op jit(solution)/shard_map/ppermute | solution.py:16
  203.1 11.6 %collective-permute-start.16 = (bf16[128,512]{1,0:T(8,128)(2,1)S(1)}, bf16[128,512]{1,0:T(8,128)(2,1)S(1)}, u32[]{:S(2)}, u32[]{:S(2)}) collective-permute-start(bf16[128,512]{1,0:T(8,128)(2,1)S(1)} %fusion.21.refs_0_), channel_id=1, source_target_pairs={{0,2},{1,3},{2,0},{3,1},{4,6},{5,7},{6,4},{7,5},{8,10},{9,11},{10,... | collective-permute-start | bytes 393224 | tf_op jit(solution)/shard_map/ppermute | solution.py:16
  214.8 7.1 %collective-permute-start.19 = (bf16[128,512]{1,0:T(8,128)(2,1)S(1)}, bf16[128,512]{1,0:T(8,128)(2,1)S(1)}, u32[]{:S(2)}, u32[]{:S(2)}) collective-permute-start(bf16[128,512]{1,0:T(8,128)(2,1)S(1)} %get-tuple-element.88), channel_id=1, source_target_pairs={{0,2},{1,3},{2,0},{3,1},{4,6},{5,7},{6,4},{7,5},{8,10},{9,11},{10,... | collective-permute-start | bytes 393224 | tf_op jit(solution)/shard_map/ppermute | solution.py:16
  214.8 12.9 %collective-permute-start.20 = (bf16[128,512]{1,0:T(8,128)(2,1)S(1)}, bf16[128,512]{1,0:T(8,128)(2,1)S(1)}, u32[]{:S(2)}, u32[]{:S(2)}) collective-permute-start(bf16[128,512]{1,0:T(8,128)(2,1)S(1)} %get-tuple-element.89), channel_id=1, source_target_pairs={{0,4},{1,5},{2,6},{3,7},{4,0},{5,1},{6,2},{7,3},{8,12},{9,13},{10,... | collective-permute-start | bytes 393224 | tf_op jit(solution)/shard_map/ppermute | solution.py:16
  217.7 10.0 %collective-permute-start.21 = (bf16[128,512]{1,0:T(8,128)(2,1)S(1)}, bf16[128,512]{1,0:T(8,128)(2,1)S(1)}, u32[]{:S(2)}, u32[]{:S(2)}) collective-permute-start(bf16[128,512]{1,0:T(8,128)(2,1)S(1)} %get-tuple-element.90), channel_id=1, source_target_pairs={{0,6},{1,7},{2,4},{3,5},{4,2},{5,3},{6,0},{7,1},{8,14},{9,15},{10,... | collective-permute-start | bytes 393224 | tf_op jit(solution)/shard_map/ppermute | solution.py:16
  230.1 22.4 %all-to-all-start.3 = ((bf16[4,400,512]{2,1,0:T(8,128)(2,1)}), bf16[4,400,512]{2,1,0:T(8,128)(2,1)}, u32[]{:S(2)}, u32[]{:S(2)}) async-start(bf16[4,400,512]{2,1,0:T(8,128)(2,1)} %dispatch.3), calls=%async_computation.3 | async-start | bytes 3276800 | tf_op jit(solution)/shard_map/all_to_all | solution.py:571
  234.5 8.3 %collective-permute-start.24 = (bf16[128,512]{1,0:T(8,128)(2,1)S(1)}, bf16[128,512]{1,0:T(8,128)(2,1)S(1)}, u32[]{:S(2)}, u32[]{:S(2)}) collective-permute-start(bf16[128,512]{1,0:T(8,128)(2,1)S(1)} %fusion.16.refs_0_), channel_id=1, source_target_pairs={{0,6},{1,7},{2,4},{3,5},{4,2},{5,3},{6,0},{7,1},{8,14},{9,15},{10,... | collective-permute-start | bytes 393224 | tf_op jit(solution)/shard_map/ppermute | solution.py:16
  236.9 10.8 %collective-permute-start.23 = (bf16[128,512]{1,0:T(8,128)(2,1)S(1)}, bf16[128,512]{1,0:T(8,128)(2,1)S(1)}, u32[]{:S(2)}, u32[]{:S(2)}) collective-permute-start(bf16[128,512]{1,0:T(8,128)(2,1)S(1)} %fusion.16.refs_0_), channel_id=1, source_target_pairs={{0,4},{1,5},{2,6},{3,7},{4,0},{5,1},{6,2},{7,3},{8,12},{9,13},{10,... | collective-permute-start | bytes 393224 | tf_op jit(solution)/shard_map/ppermute | solution.py:16
  238.1 9.6 %collective-permute-start.22 = (bf16[128,512]{1,0:T(8,128)(2,1)S(1)}, bf16[128,512]{1,0:T(8,128)(2,1)S(1)}, u32[]{:S(2)}, u32[]{:S(2)}) collective-permute-start(bf16[128,512]{1,0:T(8,128)(2,1)S(1)} %fusion.16.refs_0_), channel_id=1, source_target_pairs={{0,2},{1,3},{2,0},{3,1},{4,6},{5,7},{6,4},{7,5},{8,10},{9,11},{10,... | collective-permute-start | bytes 393224 | tf_op jit(solution)/shard_map/ppermute | solution.py:16
  252.4 3.8 %collective-permute-start.25 = (bf16[4,400,512]{2,1,0:T(8,128)(2,1)}, bf16[4,400,512]{2,1,0:T(8,128)(2,1)S(1)}, u32[]{:S(2)}, u32[]{:S(2)}) collective-permute-start(bf16[4,400,512]{2,1,0:T(8,128)(2,1)} %all-to-all-done.3.own_ref), channel_id=1, source_target_pairs={{0,1},{1,0},{2,3},{3,2},{4,5},{5,4},{6,7},{7,6},{8,9},{9,8},{10,11... | collective-permute-start | bytes 4915208 | tf_op jit(solution)/shard_map/ppermute | solution.py:16
  252.4 24.4 %all-to-all-start.2 = ((bf16[4,400,512]{2,1,0:T(8,128)(2,1)}), bf16[4,400,512]{2,1,0:T(8,128)(2,1)S(1)}, u32[]{:S(2)}, u32[]{:S(2)}) async-start(bf16[4,400,512]{2,1,0:T(8,128)(2,1)} %dispatch.2), calls=%async_computation.2 | async-start | bytes 3276800 | tf_op jit(solution)/shard_map/all_to_all | solution.py:571
  256.2 1.2 copy-start.14
  276.9 3.5 %copy-start.3 = (bf16[4,400,512]{2,1,0:T(8,128)(2,1)}, bf16[4,400,512]{2,1,0:T(8,128)(2,1)S(1)}, u32[]{:S(2)}) copy-start(bf16[4,400,512]{2,1,0:T(8,128)(2,1)S(1)} %all-to-all-done.2.own_ref) | copy-start | bytes 4915204
  276.9 3.5 %collective-permute-start.26 = (bf16[4,400,512]{2,1,0:T(8,128)(2,1)S(1)}, bf16[4,400,512]{2,1,0:T(8,128)(2,1)S(1)}, u32[]{:S(2)}, u32[]{:S(2)}) collective-permute-start(bf16[4,400,512]{2,1,0:T(8,128)(2,1)S(1)} %all-to-all-done.2.own_ref), channel_id=1, source_target_pairs={{0,1},{1,0},{2,3},{3,2},{4,5},{5,4},{6,7},{7,6},{8,9},{9,8},{10,11... | collective-permute-start | bytes 4915208 | tf_op jit(solution)/shard_map/ppermute | solution.py:16
  280.4 1.2 copy-start.4

commit v2 on v1

--- a/solution.py
+++ b/solution.py
@@ -63,37 +63,36 @@
         out_ref[b] = jnp.where(last, filled, signs)
 
 
-def pack_kernel(c, flip, position_ref, branch_ref, low_out, high_out, sems):
-    others, half, part = low_out.shape
-    expert = position_ref[0]
-    copies = []
-    for j in range(others):
-        low = 2 * j + (expert % 2 ^ flip)
-        high = j + others * (expert // others ^ flip)
-        for h, (place, out) in enumerate(((low, low_out), (high, high_out))):
-            columns = pl.ds(pl.multiple_of((place * CHUNKS + c) * part, 128), part)
-            source = branch_ref.at[pl.ds(h * half, half), columns]
-            copies.append(pltpu.make_async_copy(source, out.at[j], sems.at[2 * j + h]))
-    for copy in copies:
-        copy.start()
-    for copy in copies:
-        copy.wait()
+def pack_kernel(position_ref, low_ref, high_ref, low_out, high_out):
+    low_out[0] = low_ref[...]
+    high_out[0] = high_ref[...]
 
 
 def pack(position, branch, c, flip, experts):
+    half = branch.shape[0] // 2
+    part = branch.shape[1] // experts // CHUNKS
     others = experts // 2
-    shape = (others, branch.shape[0] // 2, branch.shape[1] // experts // CHUNKS)
-    source_spec = pl.BlockSpec(memory_space=pltpu.HBM)
-    spec = pl.BlockSpec(memory_space=pl.ANY)
+
+    def low(j, position_ref):
+        return (0, (2 * j + (position_ref[0] % 2 ^ flip)) * CHUNKS + c)
+
+    def high(j, position_ref):
+        return (1, (j + others * (position_ref[0] // others ^ flip)) * CHUNKS + c)
+
+    block = pl.BlockSpec((1, half, part), lambda j, position_ref: (j, 0, 0))
+    shape = jax.ShapeDtypeStruct((others, half, part), jnp.bfloat16)
     return pl.pallas_call(
-        functools.partial(pack_kernel, c, flip),
-        out_shape=(jax.ShapeDtypeStruct(shape, jnp.bfloat16),) * 2,
-        in_specs=[smem(), source_spec],
-        out_specs=(spec, spec),
-        scratch_shapes=[pltpu.SemaphoreType.DMA((2 * others,))],
+        pack_kernel,
+        out_shape=(shape, shape),
+        grid_spec=pltpu.PrefetchScalarGridSpec(
+            num_scalar_prefetch=1,
+            grid=(others,),
+            in_specs=[pl.BlockSpec((half, part), low), pl.BlockSpec((half, part), high)],
+            out_specs=(block, block),
+        ),
         compiler_params=params(61),
         name="pack",
-    )(position, branch)
+    )(position, branch, branch)
 
 
 def join_kernel(*refs):

time: 315 us -> 199 us (0.63)
  Pallas kernels: 189 us -> 65.9 us
  waiting for transfers between devices: 55.4 us -> 60.4 us
    pallas_call x4, Pallas kernels: 134 us -> 11.1 us  [pack(): pl.pallas_call(pack_kernel, out_shape=(shape, shape), grid_spec=pltpu.Pre...]
    ppermute x27, waiting for transfers between devices: 43.7 us -> 48.6 us  [exchange(): return lax.ppermute(value, axis, [(i, i ^ offset) for i in range(size)])]
  transfers between devices with their start and end apart: 31 -> 31, of which waited for: 13 -> 21; matrix products, arithmetic and copies ran while one was open for 4% -> 6% of each run, Pallas kernels for 38% -> 14%
where the time goes in v2:
time: 199 us; the launch traced here: 198 us
  Pallas kernels  65.9 us (33%)
  waiting for transfers between devices  60.4 us (30%)
  starting transfers between devices  50.1 us (25%)
  other arithmetic  12.6 us (6%)
  local copies, waits for them, and re-layouts  4.78 us (2%)
  matrix products  2.78 us (1%)
    ppermute x27, waiting for transfers between devices, exchange(): return lax.ppermute(value, axis, [(i, i ^ offset) for i in range(size)])  48.6 us
    pallas_call x1, Pallas kernels, per_device(): pl.pallas_call(functools.partial(late_kernel, float(width), tiles), out_s...  32.1 us
    ppermute x27, starting transfers between devices, exchange(): return lax.ppermute(value, axis, [(i, i ^ offset) for i in range(size)])  31.9 us
    pallas_call x1, Pallas kernels, per_device(): pl.pallas_call(functools.partial(early_kernel, tiles), out_shape=(sums, s...  15 us
    pallas_call x4, Pallas kernels, pack(): pl.pallas_call(pack_kernel, out_shape=(shape, shape), grid_spec=pltpu.Pre...  11.1 us
    all_to_all x2, starting transfers between devices, to_experts(): lax.all_to_all(slots[c], 'expert', split_axis=0, concat_axis=0, tiled=True)  8.14 us
    all_to_all x2, waiting for transfers between devices, to_experts(): lax.all_to_all(slots[c], 'expert', split_axis=0, concat_axis=0, tiled=True)  7.04 us
    convert_element_type x4, other arithmetic, branch_sends(): stacked.append(held[c, h](chosen).astype(jnp.bfloat16))  6.86 us
  transfers between devices with their start and end apart: 31, of which 21 were waited for; matrix products, arithmetic and copies ran while one was open for 6% of the time, Pallas kernels for 14%

profile of v2, /device:TPU:0, one launch (start us, length us, event | category | flops | bytes accessed | tf_op | source)
XLA Modules:
  0.0 197.7 jit_solution(9897529880127606743)
XLA Ops:
  0.6 5.2 %all-to-all-start = ((bf16[4,32,1024]{2,1,0:T(8,128)(2,1)}), bf16[4,32,1024]{2,1,0:T(8,128)(2,1)S(1)}, u32[]{:S(2)}, u32[]{:S(2)}) async-start(bf16[4,32,1024]{2,1,0:T(8,128)(2,1)} %bitcast.114), calls=%async_computation | async-start | bytes 524288 | tf_op jit(solution)/shard_map/all_to_all | solution.py:440
  6.5 4.7 %all-to-all-done.shares_ref = bf16[4,32,1024]{2,1,0:T(8,128)(2,1)S(1)} async-done(((bf16[4,32,1024]{2,1,0:T(8,128)(2,1)}), bf16[4,32,1024]{2,1,0:T(8,128)(2,1)S(1)}, u32[]{:S(2)}, u32[]{:S(2)}) %all-to-all-start) | async-done | bytes 262176 | tf_op jit(solution)/shard_map/all_to_all | solution.py:440
  11.2 2.8 %pack.5 = (bf16[2,256,512]{2,1,0:T(8,128)(2,1)}, bf16[2,256,512]{2,1,0:T(8,128)(2,1)}) custom-call(s32[3]{0:T(128)} %pad_add_fusion.position_ref, bf16[512,4096]{1,0:T(8,128)(2,1)} %bitcast.101, bf16[512,4096]{1,0:T(8,128)(2,1)} %bitcast.102), custom_call_target="tpu_custom_call" | custom-call | tf_op jit(solution)/shard_map/pack/pallas_call | solution.py:84
  14.0 1.3 collective-permute-start
  15.9 0.8 spread.1
  16.7 4.9 %all-to-all-start.1 = ((bf16[8,48,512]{2,1,0:T(8,128)(2,1)}), bf16[8,48,512]{2,1,0:T(8,128)(2,1)S(1)}, u32[]{:S(2)}, u32[]{:S(2)}) async-start(bf16[8,48,512]{2,1,0:T(8,128)(2,1)} %spread.1), calls=%async_computation.1 | async-start | bytes 786432 | tf_op jit(solution)/shard_map/all_to_all | solution.py:457
  21.6 2.7 %pack.4 = (bf16[2,256,512]{2,1,0:T(8,128)(2,1)}, bf16[2,256,512]{2,1,0:T(8,128)(2,1)}) custom-call(s32[3]{0:T(128)} %pad_add_fusion.position_ref, bf16[512,4096]{1,0:T(8,128)(2,1)} %bitcast.103, bf16[512,4096]{1,0:T(8,128)(2,1)} %bitcast.104), custom_call_target="tpu_custom_call" | custom-call | tf_op jit(solution)/shard_map/pack/pallas_call | solution.py:84
  24.3 2.2 %collective-permute-done = bf16[2,256,512]{2,1,0:T(8,128)(2,1)S(1)} collective-permute-done((bf16[2,256,512]{2,1,0:T(8,128)(2,1)}, bf16[2,256,512]{2,1,0:T(8,128)(2,1)S(1)}, u32[]{:S(2)}, u32[]{:S(2)}) %collective-permute-start) | collective-permute-done | bytes 524320 | tf_op jit(solution)/shard_map/ppermute | solution.py:16
  26.5 1.0 collective-permute-done.1
  27.5 1.7 add_convert_fusion.2
  29.2 0.8 collective-permute-start.3
  29.9 1.7 add_convert_fusion.3
  31.7 1.5 collective-permute-start.2
  33.2 2.8 %pack.6 = (bf16[2,256,512]{2,1,0:T(8,128)(2,1)}, bf16[2,256,512]{2,1,0:T(8,128)(2,1)}) custom-call(s32[3]{0:T(128)} %pad_add_fusion.position_ref, bf16[512,4096]{1,0:T(8,128)(2,1)} %bitcast.105, bf16[512,4096]{1,0:T(8,128)(2,1)} %bitcast.106), custom_call_target="tpu_custom_call" | custom-call | tf_op jit(solution)/shard_map/pack/pallas_call | solution.py:84
  36.0 2.3 %collective-permute-done.2 = bf16[1,256,512]{2,1,0:T(8,128)(2,1)} collective-permute-done((bf16[1,256,512]{2,1,0:T(8,128)(2,1)}, bf16[1,256,512]{2,1,0:T(8,128)(2,1)}, u32[]{:S(2)}, u32[]{:S(2)}) %collective-permute-start.2) | collective-permute-done | bytes 262176 | tf_op jit(solution)/shard_map/ppermute | solution.py:16
  38.4 1.3 collective-permute-start.6
  39.7 4.3 %collective-permute-start.5 = (bf16[8,32,512]{2,1,0:T(8,128)(2,1)S(1)}, bf16[8,32,512]{2,1,0:T(8,128)(2,1)S(1)}, u32[]{:S(2)}, u32[]{:S(2)}) collective-permute-start(bf16[8,32,512]{2,1,0:T(8,128)(2,1)S(1)} %slice.18), channel_id=1, source_target_pairs={{0,16},{8,24},{16,0},{24,8},{1,17},{9,25},{17,1},{25,9},{2,18},{10... | collective-permute-start | bytes 786440 | tf_op jit(solution)/shard_map/ppermute | solution.py:16
  44.3 0.8 signs.1
  45.1 1.3 add_bitcast_fusion.2
  46.6 0.8 collective-permute-done.6
  47.3 3.1 %collective-permute-done.5 = bf16[8,32,512]{2,1,0:T(8,128)(2,1)S(1)} collective-permute-done((bf16[8,32,512]{2,1,0:T(8,128)(2,1)S(1)}, bf16[8,32,512]{2,1,0:T(8,128)(2,1)S(1)}, u32[]{:S(2)}, u32[]{:S(2)}) %collective-permute-start.5) | collective-permute-done | bytes 262176 | tf_op jit(solution)/shard_map/ppermute | solution.py:16
  50.4 1.1 collective-permute-done.4
  52.6 1.2 collective-permute-start.7
  54.4 2.7 %pack.7 = (bf16[2,256,512]{2,1,0:T(8,128)(2,1)}, bf16[2,256,512]{2,1,0:T(8,128)(2,1)}) custom-call(s32[3]{0:T(128)} %pad_add_fusion.position_ref, bf16[512,4096]{1,0:T(8,128)(2,1)} %bitcast.107, bf16[512,4096]{1,0:T(8,128)(2,1)} %bitcast.108), custom_call_target="tpu_custom_call" | custom-call | tf_op jit(solution)/shard_map/pack/pallas_call | solution.py:84
  57.2 0.8 copy-done.5
  58.0 1.5 convert_add_fusion.1
  59.5 0.8 fusion.24
  60.3 3.7 %collective-permute-start.14 = (bf16[128,512]{1,0:T(8,128)(2,1)}, bf16[128,512]{1,0:T(8,128)(2,1)S(1)}, u32[]{:S(2)}, u32[]{:S(2)}) collective-permute-start(bf16[128,512]{1,0:T(8,128)(2,1)} %get-tuple-element.111), channel_id=1, source_target_pairs={{0,6},{1,7},{2,4},{3,5},{4,2},{5,3},{6,0},{7,1},{8,14},{9,15},{10,... | collective-permute-start | bytes 393224 | tf_op jit(solution)/shard_map/ppermute | solution.py:16
  64.7 2.6 %collective-permute-done.7 = bf16[2,256,512]{2,1,0:T(8,128)(2,1)} collective-permute-done((bf16[2,256,512]{2,1,0:T(8,128)(2,1)}, bf16[2,256,512]{2,1,0:T(8,128)(2,1)}, u32[]{:S(2)}, u32[]{:S(2)}) %collective-permute-start.7) | collective-permute-done | bytes 524320 | tf_op jit(solution)/shard_map/ppermute | solution.py:16
  67.3 0.8 collective-permute-done.8
  68.2 1.7 add_convert_fusion
  69.9 0.9 collective-permute-start.11
  70.8 1.7 add_convert_fusion.1
  72.5 1.4 collective-permute-start.10
  73.9 1.1 collective-permute-done.13
  75.7 1.1 fusion.21.refs_0_
  76.8 0.9 collective-permute-done.11
  77.6 2.4 %collective-permute-done.10 = bf16[1,256,512]{2,1,0:T(8,128)(2,1)} collective-permute-done((bf16[1,256,512]{2,1,0:T(8,128)(2,1)}, bf16[1,256,512]{2,1,0:T(8,128)(2,1)}, u32[]{:S(2)}, u32[]{:S(2)}) %collective-permute-start.10) | collective-permute-done | bytes 262176 | tf_op jit(solution)/shard_map/ppermute | solution.py:16
  80.1 1.1 add_bitcast_fusion
  81.2 1.2 add_bitcast_fusion.1
  83.1 3.8 %collective-permute-start.18 = (bf16[128,512]{1,0:T(8,128)(2,1)S(1)}, bf16[128,512]{1,0:T(8,128)(2,1)S(1)}, u32[]{:S(2)}, u32[]{:S(2)}) collective-permute-start(bf16[128,512]{1,0:T(8,128)(2,1)S(1)} %fusion.21.refs_0_), channel_id=1, source_target_pairs={{0,6},{1,7},{2,4},{3,5},{4,2},{5,3},{6,0},{7,1},{8,14},{9,15},{10,... | collective-permute-start | bytes 393224 | tf_op jit(solution)/shard_map/ppermute | solution.py:16
  88.1 3.4 %collective-permute-done.18.refs_3_ = bf16[128,512]{1,0:T(8,128)(2,1)S(1)} collective-permute-done((bf16[128,512]{1,0:T(8,128)(2,1)S(1)}, bf16[128,512]{1,0:T(8,128)(2,1)S(1)}, u32[]{:S(2)}, u32[]{:S(2)}) %collective-permute-start.18) | collective-permute-done | bytes 131104 | tf_op jit(solution)/shard_map/ppermute | solution.py:16
  91.4 6.9 %collective-permute-done.17.refs_2_ = bf16[128,512]{1,0:T(8,128)(2,1)S(1)} collective-permute-done((bf16[128,512]{1,0:T(8,128)(2,1)S(1)}, bf16[128,512]{1,0:T(8,128)(2,1)S(1)}, u32[]{:S(2)}, u32[]{:S(2)}) %collective-permute-start.17) | collective-permute-done | bytes 131104 | tf_op jit(solution)/shard_map/ppermute | solution.py:16
  98.4 3.1 %collective-permute-start.20 = (bf16[128,512]{1,0:T(8,128)(2,1)S(1)}, bf16[128,512]{1,0:T(8,128)(2,1)S(1)}, u32[]{:S(2)}, u32[]{:S(2)}) collective-permute-start(bf16[128,512]{1,0:T(8,128)(2,1)S(1)} %get-tuple-element.89), channel_id=1, source_target_pairs={{0,4},{1,5},{2,6},{3,7},{4,0},{5,1},{6,2},{7,3},{8,12},{9,13},{10,... | collective-permute-start | bytes 393224 | tf_op jit(solution)/shard_map/ppermute | solution.py:16
  101.5 1.2 collective-permute-start.21
  102.7 1.1 join.1
  103.8 1.8 collective-permute-done.19
  105.6 5.9 %collective-permute-done.20 = bf16[128,512]{1,0:T(8,128)(2,1)S(1)} collective-permute-done((bf16[128,512]{1,0:T(8,128)(2,1)S(1)}, bf16[128,512]{1,0:T(8,128)(2,1)S(1)}, u32[]{:S(2)}, u32[]{:S(2)}) %collective-permute-start.20) | collective-permute-done | bytes 131104 | tf_op jit(solution)/shard_map/ppermute | solution.py:16
  111.6 2.3 %dispatch.3 = bf16[4,400,512]{2,1,0:T(8,128)(2,1)} custom-call(s32[3]{0:T(128)S(1)} %copy-done.2, s32[8,4,128]{2,1,0:T(4,128)S(1)} %bitcast.96, bf16[16,1024]{1,0:T(8,128)(2,1)S(1)} %fusion.30.extra_ref, bf16[128,512]{1,0:T(8,128)(2,1)S(1)} %fusion.21.refs_0_, bf16[128,512]{1,0:T(8,128)(2,1)S(1)} %collective-permute-done.16.refs_1_, ...), custom_call_target="tpu_custom_call" | custom-call | tf_op jit(solution)/shard_map/dispatch/pallas_call | solution.py:522
  113.9 4.4 %all-to-all-start.3 = ((bf16[4,400,512]{2,1,0:T(8,128)(2,1)}), bf16[4,400,512]{2,1,0:T(8,128)(2,1)}, u32[]{:S(2)}, u32[]{:S(2)}) async-start(bf16[4,400,512]{2,1,0:T(8,128)(2,1)} %dispatch.3), calls=%async_computation.3 | async-start | bytes 3276800 | tf_op jit(solution)/shard_map/all_to_all | solution.py:570
  118.3 2.4 %collective-permute-start.24 = (bf16[128,512]{1,0:T(8,128)(2,1)S(1)}, bf16[128,512]{1,0:T(8,128)(2,1)S(1)}, u32[]{:S(2)}, u32[]{:S(2)}) collective-permute-start(bf16[128,512]{1,0:T(8,128)(2,1)S(1)} %fusion.16.refs_0_), channel_id=1, source_target_pairs={{0,6},{1,7},{2,4},{3,5},{4,2},{5,3},{6,0},{7,1},{8,14},{9,15},{10,... | collective-permute-start | bytes 393224 | tf_op jit(solution)/shard_map/ppermute | solution.py:16
  120.7 1.2 collective-permute-start.23
  121.9 0.9 collective-permute-start.22
  122.8 3.8 %collective-permute-done.24.refs_3_ = bf16[128,512]{1,0:T(8,128)(2,1)S(1)} collective-permute-done((bf16[128,512]{1,0:T(8,128)(2,1)S(1)}, bf16[128,512]{1,0:T(8,128)(2,1)S(1)}, u32[]{:S(2)}, u32[]{:S(2)}) %collective-permute-start.24) | collective-permute-done | bytes 131104 | tf_op jit(solution)/shard_map/ppermute | solution.py:16
  126.6 4.9 %collective-permute-done.23.refs_2_ = bf16[128,512]{1,0:T(8,128)(2,1)S(1)} collective-permute-done((bf16[128,512]{1,0:T(8,128)(2,1)S(1)}, bf16[128,512]{1,0:T(8,128)(2,1)S(1)}, u32[]{:S(2)}, u32[]{:S(2)}) %collective-permute-start.23) | collective-permute-done | bytes 131104 | tf_op jit(solution)/shard_map/ppermute | solution.py:16
  131.5 2.3 %dispatch.2 = bf16[4,400,512]{2,1,0:T(8,128)(2,1)} custom-call(s32[3]{0:T(128)S(1)} %copy-done.2, s32[8,4,128]{2,1,0:T(4,128)S(1)} %bitcast.97, bf16[16,1024]{1,0:T(8,128)(2,1)S(1)} %fusion.30.extra_ref, bf16[128,512]{1,0:T(8,128)(2,1)S(1)} %fusion.16.refs_0_, bf16[128,512]{1,0:T(8,128)(2,1)S(1)} %collective-permute-done.22.refs_1_, ...), custom_call_target="tpu_custom_call" | custom-call | tf_op jit(solution)/shard_map/dispatch/pallas_call | solution.py:522
  133.8 2.5 %all-to-all-done.3.own_ref = bf16[4,400,512]{2,1,0:T(8,128)(2,1)} async-done(((bf16[4,400,512]{2,1,0:T(8,128)(2,1)}), bf16[4,400,512]{2,1,0:T(8,128)(2,1)}, u32[]{:S(2)}, u32[]{:S(2)}) %all-to-all-start.3) | async-done | bytes 1638432 | tf_op jit(solution)/shard_map/all_to_all | solution.py:570
  136.3 3.8 %all-to-all-start.2 = ((bf16[4,400,512]{2,1,0:T(8,128)(2,1)}), bf16[4,400,512]{2,1,0:T(8,128)(2,1)S(1)}, u32[]{:S(2)}, u32[]{:S(2)}) async-start(bf16[4,400,512]{2,1,0:T(8,128)(2,1)} %dispatch.2), calls=%async_computation.2 | async-start | bytes 3276800 | tf_op jit(solution)/shard_map/all_to_all | solution.py:570
  140.0 1.2 copy-done.14
  141.2 15.0 %early.1 = (f32[768,1024]{1,0:T(8,128)}, f32[768,1024]{1,0:T(8,128)}, f32[768,16]{1,0:T(8,128)}, bf16[4,512,768]{2,1,0:T(8,128)(2,1)}) custom-call(bf16[4,400,512]{2,1,0:T(8,128)(2,1)} %all-to-all-done.3.own_ref, bf16[4,400,512]{2,1,0:T(8,128)(2,1)} %copy-done.14, bf16[4,2,512,1024]{3,2,1,0:T(8,128)(2,1)} %bitcast.109, bf16[4,2,512,1024]{3,2,1,0:T(8,128)(2,1)} %bitcast.111), custom_call_target="tpu_custom_call" | custom-call | flops 6442450944 | bytes 8388608 | tf_op jit(solution)/shard_map/early/pallas_call | solution.py:582
  156.2 4.5 %all-to-all-done.2.own_ref = bf16[4,400,512]{2,1,0:T(8,128)(2,1)S(1)} async-done(((bf16[4,400,512]{2,1,0:T(8,128)(2,1)}), bf16[4,400,512]{2,1,0:T(8,128)(2,1)S(1)}, u32[]{:S(2)}, u32[]{:S(2)}) %all-to-all-start.2) | async-done | bytes 1638432 | tf_op jit(solution)/shard_map/all_to_all | solution.py:570
  160.7 3.5 %collective-permute-done.26.other_ref = bf16[4,400,512]{2,1,0:T(8,128)(2,1)S(1)} collective-permute-done((bf16[4,400,512]{2,1,0:T(8,128)(2,1)S(1)}, bf16[4,400,512]{2,1,0:T(8,128)(2,1)S(1)}, u32[]{:S(2)}, u32[]{:S(2)}) %collective-permute-start.26) | collective-permute-done | bytes 1638432 | tf_op jit(solution)/shard_map/ppermute | solution.py:16
  164.2 1.2 copy-done.4
  165.5 32.1 %late.1 = (bf16[4,2,96,1024]{3,2,1,0:T(8,128)(2,1)}, bf16[4,1024,1024]{2,1,0:T(8,128)(2,1)}, bf16[4,1024,1024]{2,1,0:T(8,128)(2,1)}) custom-call(s32[3]{0:T(128)} %pad_add_fusion.position_ref, bf16[4,400,512]{2,1,0:T(8,128)(2,1)} %copy-done.3, bf16[4,400,512]{2,1,0:T(8,128)(2,1)} %copy-done.4, bf16[4,512,768]{2,1,0:T(8,128)(2,1)} %get-tuple-element.103.turned_ref, ...), custom_call_target="tpu_custom_call" | custom-call | tf_op jit(solution)/shard_map/late/pallas_call | solution.py:621
  (72 shorter events, 6.8 us)
Async XLA Ops:
  0.6 10.5 %all-to-all-start = ((bf16[4,32,1024]{2,1,0:T(8,128)(2,1)}), bf16[4,32,1024]{2,1,0:T(8,128)(2,1)S(1)}, u32[]{:S(2)}, u32[]{:S(2)}) async-start(bf16[4,32,1024]{2,1,0:T(8,128)(2,1)} %bitcast.114), calls=%async_computation | async-start | bytes 524288 | tf_op jit(solution)/shard_map/all_to_all | solution.py:440
  11.2 4.7 %copy-start.15 = (s32[128,2]{0,1:T(2,128)S(1)}, s32[128,2]{0,1:T(2,128)}, u32[]{:S(2)}) copy-start(s32[128,2]{0,1:T(2,128)} %param.17) | copy-start | bytes 3076
  11.2 4.7 %copy-start.16 = (s32[128,2]{0,1:T(2,128)S(1)}, s32[128,2]{0,1:T(2,128)}, u32[]{:S(2)}) copy-start(s32[128,2]{0,1:T(2,128)} %param.18) | copy-start | bytes 3076
  14.0 12.5 %collective-permute-start = (bf16[2,256,512]{2,1,0:T(8,128)(2,1)}, bf16[2,256,512]{2,1,0:T(8,128)(2,1)S(1)}, u32[]{:S(2)}, u32[]{:S(2)}) collective-permute-start(bf16[2,256,512]{2,1,0:T(8,128)(2,1)} %get-tuple-element.59), channel_id=1, source_target_pairs={{0,8},{8,0},{16,24},{24,16},{1,9},{9,1},{17,25},{25,17},{2,10},{10... | collective-permute-start | bytes 1572872 | tf_op jit(solution)/shard_map/ppermute | solution.py:16
  15.3 12.2 %collective-permute-start.1 = (bf16[2,256,512]{2,1,0:T(8,128)(2,1)}, bf16[2,256,512]{2,1,0:T(8,128)(2,1)S(1)}, u32[]{:S(2)}, u32[]{:S(2)}) collective-permute-start(bf16[2,256,512]{2,1,0:T(8,128)(2,1)} %get-tuple-element.60), channel_id=1, source_target_pairs={{0,16},{8,24},{16,0},{24,8},{1,17},{9,25},{17,1},{25,9},{2,18},{10... | collective-permute-start | bytes 1572872 | tf_op jit(solution)/shard_map/ppermute | solution.py:16
  16.7 19.3 %all-to-all-start.1 = ((bf16[8,48,512]{2,1,0:T(8,128)(2,1)}), bf16[8,48,512]{2,1,0:T(8,128)(2,1)S(1)}, u32[]{:S(2)}, u32[]{:S(2)}) async-start(bf16[8,48,512]{2,1,0:T(8,128)(2,1)} %spread.1), calls=%async_computation.1 | async-start | bytes 786432 | tf_op jit(solution)/shard_map/all_to_all | solution.py:457
  29.2 6.8 %collective-permute-start.3 = (bf16[1,256,512]{2,1,0:T(8,128)(2,1)}, bf16[1,256,512]{2,1,0:T(8,128)(2,1)S(1)}, u32[]{:S(2)}, u32[]{:S(2)}) collective-permute-start(bf16[1,256,512]{2,1,0:T(8,128)(2,1)} %add_convert_fusion.2), channel_id=1, source_target_pairs={{0,8},{8,0},{16,24},{24,16},{1,9},{9,1},{17,25},{25,17},{2,10},{10... | collective-permute-start | bytes 786440 | tf_op jit(solution)/shard_map/ppermute | solution.py:16
  31.7 6.7 %collective-permute-start.2 = (bf16[1,256,512]{2,1,0:T(8,128)(2,1)}, bf16[1,256,512]{2,1,0:T(8,128)(2,1)}, u32[]{:S(2)}, u32[]{:S(2)}) collective-permute-start(bf16[1,256,512]{2,1,0:T(8,128)(2,1)} %add_convert_fusion.3), channel_id=1, source_target_pairs={{0,16},{8,24},{16,0},{24,8},{1,17},{9,25},{17,1},{25,9},{2,18},{10... | collective-permute-start | bytes 786440 | tf_op jit(solution)/shard_map/ppermute | solution.py:16
  33.2 11.1 %copy-start.1 = (s32[3]{0:T(128)S(1)}, s32[3]{0:T(128)}, u32[]{:S(2)}) copy-start(s32[3]{0:T(128)} %pad_add_fusion.position_ref) | copy-start | bytes 40
  33.2 12.0 %copy-start.8 = (bf16[2,256,512]{2,1,0:T(8,128)(2,1)S(1)}, bf16[2,256,512]{2,1,0:T(8,128)(2,1)}, u32[]{:S(2)}) copy-start(bf16[2,256,512]{2,1,0:T(8,128)(2,1)} %get-tuple-element.57) | copy-start | bytes 1572868
  33.2 12.0 %copy-start.9 = (bf16[2,256,512]{2,1,0:T(8,128)(2,1)S(1)}, bf16[2,256,512]{2,1,0:T(8,128)(2,1)}, u32[]{:S(2)}) copy-start(bf16[2,256,512]{2,1,0:T(8,128)(2,1)} %get-tuple-element.62) | copy-start | bytes 1572868
  38.4 8.9 %collective-permute-start.6 = (bf16[8,32,512]{2,1,0:T(8,128)(2,1)S(1)}, bf16[8,32,512]{2,1,0:T(8,128)(2,1)S(1)}, u32[]{:S(2)}, u32[]{:S(2)}) collective-permute-start(bf16[8,32,512]{2,1,0:T(8,128)(2,1)S(1)} %slice.18), channel_id=1, source_target_pairs={{0,24},{8,16},{16,8},{24,0},{1,25},{9,17},{17,9},{25,1},{2,26},{10... | collective-permute-start | bytes 786440 | tf_op jit(solution)/shard_map/ppermute | solution.py:16
  39.7 10.7 %collective-permute-start.5 = (bf16[8,32,512]{2,1,0:T(8,128)(2,1)S(1)}, bf16[8,32,512]{2,1,0:T(8,128)(2,1)S(1)}, u32[]{:S(2)}, u32[]{:S(2)}) collective-permute-start(bf16[8,32,512]{2,1,0:T(8,128)(2,1)S(1)} %slice.18), channel_id=1, source_target_pairs={{0,16},{8,24},{16,0},{24,8},{1,17},{9,25},{17,1},{25,9},{2,18},{10... | collective-permute-start | bytes 786440 | tf_op jit(solution)/shard_map/ppermute | solution.py:16
  44.0 7.5 %collective-permute-start.4 = (bf16[8,32,512]{2,1,0:T(8,128)(2,1)S(1)}, bf16[8,32,512]{2,1,0:T(8,128)(2,1)S(1)}, u32[]{:S(2)}, u32[]{:S(2)}) collective-permute-start(bf16[8,32,512]{2,1,0:T(8,128)(2,1)S(1)} %slice.18), channel_id=1, source_target_pairs={{0,8},{8,0},{16,24},{24,16},{1,9},{9,1},{17,25},{25,17},{2,10},{10... | collective-permute-start | bytes 786440 | tf_op jit(solution)/shard_map/ppermute | solution.py:16
  45.1 6.4 %copy-start = (f32[8,96,16]{2,1,0:T(8,128)}, f32[8,96,16]{2,1,0:T(8,128)S(1)}, u32[]{:S(2)}) copy-start(f32[8,96,16]{2,1,0:T(8,128)S(1)} %signs.1) | copy-start | bytes 147460
  52.6 4.6 %collective-permute-start.9 = (bf16[4,128,512]{2,1,0:T(8,128)(2,1)S(1)}, bf16[4,128,512]{2,1,0:T(8,128)(2,1)S(1)}, u32[]{:S(2)}, u32[]{:S(2)}) collective-permute-start(bf16[4,128,512]{2,1,0:T(8,128)(2,1)S(1)} %convolution_convert_fusion.1), channel_id=1, source_target_pairs={{0,1},{1,0},{2,3},{3,2},{4,5},{5,4},{6,7},{7,6},{8,9},{9,8},{10,11... | collective-permute-start | bytes 1572872 | tf_op jit(solution)/shard_map/ppermute | solution.py:16
  52.6 14.7 %collective-permute-start.7 = (bf16[2,256,512]{2,1,0:T(8,128)(2,1)}, bf16[2,256,512]{2,1,0:T(8,128)(2,1)}, u32[]{:S(2)}, u32[]{:S(2)}) collective-permute-start(bf16[2,256,512]{2,1,0:T(8,128)(2,1)} %get-tuple-element.71), channel_id=1, source_target_pairs={{0,8},{8,0},{16,24},{24,16},{1,9},{9,1},{17,25},{25,17},{2,10},{10... | collective-permute-start | bytes 1572872 | tf_op jit(solution)/shard_map/ppermute | solution.py:16
  53.8 14.3 %collective-permute-start.8 = (bf16[2,256,512]{2,1,0:T(8,128)(2,1)}, bf16[2,256,512]{2,1,0:T(8,128)(2,1)}, u32[]{:S(2)}, u32[]{:S(2)}) collective-permute-start(bf16[2,256,512]{2,1,0:T(8,128)(2,1)} %get-tuple-element.72), channel_id=1, source_target_pairs={{0,16},{8,24},{16,0},{24,8},{1,17},{9,25},{17,1},{25,9},{2,18},{10... | collective-permute-start | bytes 1572872 | tf_op jit(solution)/shard_map/ppermute | solution.py:16
  57.2 16.8 %copy-start.12 = (bf16[1024]{0:T(1024)(128)(2,1)S(1)}, bf16[1024]{0:T(1024)(128)(2,1)}, u32[]{:S(2)}) copy-start(bf16[1024]{0:T(1024)(128)(2,1)} %param.13) | copy-start | bytes 6148
  57.2 18.6 %copy-start.10 = (bf16[128,1024]{1,0:T(8,128)(2,1)S(1)}, bf16[128,1024]{1,0:T(8,128)(2,1)}, u32[]{:S(2)}) copy-start(bf16[128,1024]{1,0:T(8,128)(2,1)} %param.12) | copy-start | bytes 786436
  57.2 11.0 %copy-start.7 = (bf16[2,256,512]{2,1,0:T(8,128)(2,1)S(1)}, bf16[2,256,512]{2,1,0:T(8,128)(2,1)}, u32[]{:S(2)}) copy-start(bf16[2,256,512]{2,1,0:T(8,128)(2,1)} %get-tuple-element.84) | copy-start | bytes 1572868
  57.2 13.6 %copy-start.6 = (bf16[2,256,512]{2,1,0:T(8,128)(2,1)S(1)}, bf16[2,256,512]{2,1,0:T(8,128)(2,1)}, u32[]{:S(2)}) copy-start(bf16[2,256,512]{2,1,0:T(8,128)(2,1)} %get-tuple-element.69) | copy-start | bytes 1572868
  57.2 0.8 copy-start.5
  60.3 13.7 %collective-permute-start.14 = (bf16[128,512]{1,0:T(8,128)(2,1)}, bf16[128,512]{1,0:T(8,128)(2,1)S(1)}, u32[]{:S(2)}, u32[]{:S(2)}) collective-permute-start(bf16[128,512]{1,0:T(8,128)(2,1)} %get-tuple-element.111), channel_id=1, source_target_pairs={{0,6},{1,7},{2,4},{3,5},{4,2},{5,3},{6,0},{7,1},{8,14},{9,15},{10,... | collective-permute-start | bytes 393224 | tf_op jit(solution)/shard_map/ppermute | solution.py:16
  64.0 11.1 %collective-permute-start.13 = (bf16[128,512]{1,0:T(8,128)(2,1)}, bf16[128,512]{1,0:T(8,128)(2,1)S(1)}, u32[]{:S(2)}, u32[]{:S(2)}) collective-permute-start(bf16[128,512]{1,0:T(8,128)(2,1)} %get-tuple-element.112), channel_id=1, source_target_pairs={{0,4},{1,5},{2,6},{3,7},{4,0},{5,1},{6,2},{7,3},{8,12},{9,13},{10,... | collective-permute-start | bytes 393224 | tf_op jit(solution)/shard_map/ppermute | solution.py:16
  64.0 11.1 %collective-permute-start.12 = (bf16[128,512]{1,0:T(8,128)(2,1)}, bf16[128,512]{1,0:T(8,128)(2,1)}, u32[]{:S(2)}, u32[]{:S(2)}) collective-permute-start(bf16[128,512]{1,0:T(8,128)(2,1)} %get-tuple-element.113), channel_id=1, source_target_pairs={{0,2},{1,3},{2,0},{3,1},{4,6},{5,7},{6,4},{7,5},{8,10},{9,11},{10,... | collective-permute-start | bytes 393224 | tf_op jit(solution)/shard_map/ppermute | solution.py:16
  69.9 7.8 %collective-permute-start.11 = (bf16[1,256,512]{2,1,0:T(8,128)(2,1)}, bf16[1,256,512]{2,1,0:T(8,128)(2,1)S(1)}, u32[]{:S(2)}, u32[]{:S(2)}) collective-permute-start(bf16[1,256,512]{2,1,0:T(8,128)(2,1)} %add_convert_fusion), channel_id=1, source_target_pairs={{0,8},{8,0},{16,24},{24,16},{1,9},{9,1},{17,25},{25,17},{2,10},{10... | collective-permute-start | bytes 786440 | tf_op jit(solution)/shard_map/ppermute | solution.py:16
  72.5 7.6 %collective-permute-start.10 = (bf16[1,256,512]{2,1,0:T(8,128)(2,1)}, bf16[1,256,512]{2,1,0:T(8,128)(2,1)}, u32[]{:S(2)}, u32[]{:S(2)}) collective-permute-start(bf16[1,256,512]{2,1,0:T(8,128)(2,1)} %add_convert_fusion.1), channel_id=1, source_target_pairs={{0,16},{8,24},{16,0},{24,8},{1,17},{9,25},{17,1},{25,9},{2,18},{10... | collective-permute-start | bytes 786440 | tf_op jit(solution)/shard_map/ppermute | solution.py:16
  75.1 0.6 copy-start.11
  82.4 20.3 %copy-start.13 = (bf16[1024,4]{0,1:T(4,128)(2,1)S(1)}, bf16[1024,4]{0,1:T(4,128)(2,1)}, u32[]{:S(2)}) copy-start(bf16[1024,4]{0,1:T(4,128)(2,1)} %param.14) | copy-start | bytes 24580
  83.0 28.6 %copy-start.2 = (s32[3]{0:T(128)S(1)}, s32[3]{0:T(128)}, u32[]{:S(2)}) copy-start(s32[3]{0:T(128)} %pad_add_fusion.position_ref) | copy-start | bytes 40
  83.0 4.5 %collective-permute-start.15 = (bf16[4,128,512]{2,1,0:T(8,128)(2,1)S(1)}, bf16[4,128,512]{2,1,0:T(8,128)(2,1)S(1)}, u32[]{:S(2)}, u32[]{:S(2)}) collective-permute-start(bf16[4,128,512]{2,1,0:T(8,128)(2,1)S(1)} %convolution_convert_fusion), channel_id=1, source_target_pairs={{0,1},{1,0},{2,3},{3,2},{4,5},{5,4},{6,7},{7,6},{8,9},{9,8},{10,11... | collective-permute-start | bytes 1572872 | tf_op jit(solution)/shard_map/ppermute | solution.py:16
  83.1 8.3 %collective-permute-start.18 = (bf16[128,512]{1,0:T(8,128)(2,1)S(1)}, bf16[128,512]{1,0:T(8,128)(2,1)S(1)}, u32[]{:S(2)}, u32[]{:S(2)}) collective-permute-start(bf16[128,512]{1,0:T(8,128)(2,1)S(1)} %fusion.21.refs_0_), channel_id=1, source_target_pairs={{0,6},{1,7},{2,4},{3,5},{4,2},{5,3},{6,0},{7,1},{8,14},{9,15},{10,... | collective-permute-start | bytes 393224 | tf_op jit(solution)/shard_map/ppermute | solution.py:16
  86.9 11.4 %collective-permute-start.17 = (bf16[128,512]{1,0:T(8,128)(2,1)S(1)}, bf16[128,512]{1,0:T(8,128)(2,1)S(1)}, u32[]{:S(2)}, u32[]{:S(2)}) collective-permute-start(bf16[128,512]{1,0:T(8,128)(2,1)S(1)} %fusion.21.refs_0_), channel_id=1, source_target_pairs={{0,4},{1,5},{2,6},{3,7},{4,0},{5,1},{6,2},{7,3},{8,12},{9,13},{10,... | collective-permute-start | bytes 393224 | tf_op jit(solution)/shard_map/ppermute | solution.py:16
  86.9 11.4 %collective-permute-start.16 = (bf16[128,512]{1,0:T(8,128)(2,1)S(1)}, bf16[128,512]{1,0:T(8,128)(2,1)S(1)}, u32[]{:S(2)}, u32[]{:S(2)}) collective-permute-start(bf16[128,512]{1,0:T(8,128)(2,1)S(1)} %fusion.21.refs_0_), channel_id=1, source_target_pairs={{0,2},{1,3},{2,0},{3,1},{4,6},{5,7},{6,4},{7,5},{8,10},{9,11},{10,... | collective-permute-start | bytes 393224 | tf_op jit(solution)/shard_map/ppermute | solution.py:16
  98.3 7.3 %collective-permute-start.19 = (bf16[128,512]{1,0:T(8,128)(2,1)S(1)}, bf16[128,512]{1,0:T(8,128)(2,1)S(1)}, u32[]{:S(2)}, u32[]{:S(2)}) collective-permute-start(bf16[128,512]{1,0:T(8,128)(2,1)S(1)} %get-tuple-element.88), channel_id=1, source_target_pairs={{0,2},{1,3},{2,0},{3,1},{4,6},{5,7},{6,4},{7,5},{8,10},{9,11},{10,... | collective-permute-start | bytes 393224 | tf_op jit(solution)/shard_map/ppermute | solution.py:16
  98.4 13.1 %collective-permute-start.20 = (bf16[128,512]{1,0:T(8,128)(2,1)S(1)}, bf16[128,512]{1,0:T(8,128)(2,1)S(1)}, u32[]{:S(2)}, u32[]{:S(2)}) collective-permute-start(bf16[128,512]{1,0:T(8,128)(2,1)S(1)} %get-tuple-element.89), channel_id=1, source_target_pairs={{0,4},{1,5},{2,6},{3,7},{4,0},{5,1},{6,2},{7,3},{8,12},{9,13},{10,... | collective-permute-start | bytes 393224 | tf_op jit(solution)/shard_map/ppermute | solution.py:16
  101.5 10.0 %collective-permute-start.21 = (bf16[128,512]{1,0:T(8,128)(2,1)S(1)}, bf16[128,512]{1,0:T(8,128)(2,1)S(1)}, u32[]{:S(2)}, u32[]{:S(2)}) collective-permute-start(bf16[128,512]{1,0:T(8,128)(2,1)S(1)} %get-tuple-element.90), channel_id=1, source_target_pairs={{0,6},{1,7},{2,4},{3,5},{4,2},{5,3},{6,0},{7,1},{8,14},{9,15},{10,... | collective-permute-start | bytes 393224 | tf_op jit(solution)/shard_map/ppermute | solution.py:16
  113.9 22.4 %all-to-all-start.3 = ((bf16[4,400,512]{2,1,0:T(8,128)(2,1)}), bf16[4,400,512]{2,1,0:T(8,128)(2,1)}, u32[]{:S(2)}, u32[]{:S(2)}) async-start(bf16[4,400,512]{2,1,0:T(8,128)(2,1)} %dispatch.3), calls=%async_computation.3 | async-start | bytes 3276800 | tf_op jit(solution)/shard_map/all_to_all | solution.py:570
  118.3 8.3 %collective-permute-start.24 = (bf16[128,512]{1,0:T(8,128)(2,1)S(1)}, bf16[128,512]{1,0:T(8,128)(2,1)S(1)}, u32[]{:S(2)}, u32[]{:S(2)}) collective-permute-start(bf16[128,512]{1,0:T(8,128)(2,1)S(1)} %fusion.16.refs_0_), channel_id=1, source_target_pairs={{0,6},{1,7},{2,4},{3,5},{4,2},{5,3},{6,0},{7,1},{8,14},{9,15},{10,... | collective-permute-start | bytes 393224 | tf_op jit(solution)/shard_map/ppermute | solution.py:16
  120.7 10.8 %collective-permute-start.23 = (bf16[128,512]{1,0:T(8,128)(2,1)S(1)}, bf16[128,512]{1,0:T(8,128)(2,1)S(1)}, u32[]{:S(2)}, u32[]{:S(2)}) collective-permute-start(bf16[128,512]{1,0:T(8,128)(2,1)S(1)} %fusion.16.refs_0_), channel_id=1, source_target_pairs={{0,4},{1,5},{2,6},{3,7},{4,0},{5,1},{6,2},{7,3},{8,12},{9,13},{10,... | collective-permute-start | bytes 393224 | tf_op jit(solution)/shard_map/ppermute | solution.py:16
  121.9 9.6 %collective-permute-start.22 = (bf16[128,512]{1,0:T(8,128)(2,1)S(1)}, bf16[128,512]{1,0:T(8,128)(2,1)S(1)}, u32[]{:S(2)}, u32[]{:S(2)}) collective-permute-start(bf16[128,512]{1,0:T(8,128)(2,1)S(1)} %fusion.16.refs_0_), channel_id=1, source_target_pairs={{0,2},{1,3},{2,0},{3,1},{4,6},{5,7},{6,4},{7,5},{8,10},{9,11},{10,... | collective-permute-start | bytes 393224 | tf_op jit(solution)/shard_map/ppermute | solution.py:16
  136.2 3.8 %collective-permute-start.25 = (bf16[4,400,512]{2,1,0:T(8,128)(2,1)}, bf16[4,400,512]{2,1,0:T(8,128)(2,1)S(1)}, u32[]{:S(2)}, u32[]{:S(2)}) collective-permute-start(bf16[4,400,512]{2,1,0:T(8,128)(2,1)} %all-to-all-done.3.own_ref), channel_id=1, source_target_pairs={{0,1},{1,0},{2,3},{3,2},{4,5},{5,4},{6,7},{7,6},{8,9},{9,8},{10,11... | collective-permute-start | bytes 4915208 | tf_op jit(solution)/shard_map/ppermute | solution.py:16
  136.3 24.4 %all-to-all-start.2 = ((bf16[4,400,512]{2,1,0:T(8,128)(2,1)}), bf16[4,400,512]{2,1,0:T(8,128)(2,1)S(1)}, u32[]{:S(2)}, u32[]{:S(2)}) async-start(bf16[4,400,512]{2,1,0:T(8,128)(2,1)} %dispatch.2), calls=%async_computation.2 | async-start | bytes 3276800 | tf_op jit(solution)/shard_map/all_to_all | solution.py:570
  140.0 1.2 copy-start.14
  160.7 3.5 %copy-start.3 = (bf16[4,400,512]{2,1,0:T(8,128)(2,1)}, bf16[4,400,512]{2,1,0:T(8,128)(2,1)S(1)}, u32[]{:S(2)}) copy-start(bf16[4,400,512]{2,1,0:T(8,128)(2,1)S(1)} %all-to-all-done.2.own_ref) | copy-start | bytes 4915204
  160.7 3.5 %collective-permute-start.26 = (bf16[4,400,512]{2,1,0:T(8,128)(2,1)S(1)}, bf16[4,400,512]{2,1,0:T(8,128)(2,1)S(1)}, u32[]{:S(2)}, u32[]{:S(2)}) collective-permute-start(bf16[4,400,512]{2,1,0:T(8,128)(2,1)S(1)} %all-to-all-done.2.own_ref), channel_id=1, source_target_pairs={{0,1},{1,0},{2,3},{3,2},{4,5},{5,4},{6,7},{7,6},{8,9},{9,8},{10,11... | collective-permute-start | bytes 4915208 | tf_op jit(solution)/shard_map/ppermute | solution.py:16
  164.2 1.2 copy-start.4
